TPU v7x, 256 devices: a whole 4x4x8 slice. The times are simulated.
256 devices in a mesh: fsdp: 8 (over z), rep: 32 (over x, y, core).
Axes of the slice: x: 4, y: 4, z: 8, core: 2. Of those that a mesh axis runs over, the one named last changes fastest.
Arguments:
- grads: bfloat16 [32, 8192, 512], P('rep', 'fsdp'), may hold values from -120 to 120
- errors: bfloat16 [32, 8192, 512], P('rep', 'fsdp'), may hold values from -4 to 4
- q_prev: float32 [512, 64], replicated, may hold values from -6 to 6
- weight: float32 [8192, 512], P('fsdp'), may hold values from -4 to 4
- first_moment: bfloat16 [8192, 512], P('fsdp'), may hold values from -0.59765625 to 0.59765625
- second_moment: bfloat16 [8192, 512], P('fsdp'), may hold values from 0.0029907227 to 0.029907227
Outputs:
- new_errors: bfloat16 [32, 8192, 512], P('rep', 'fsdp')
- q_next: float32 [512, 64], replicated
- new_weight: float32 [8192, 512], P('fsdp')
- new_first: bfloat16 [8192, 512], P('fsdp')
- new_second: bfloat16 [8192, 512], P('fsdp')
All inputs are finite; a program needn't handle non-finite values.
Results may differ from a plain program's by a relative error of at most 0.0018.
Values sent between devices are 32-bit elements; how exact they have to be, the bound alone decides.
No kernel may reach another device: no remote copies, remote signals or barrier semaphores. Data moves between devices by JAX's collectives and lax.ppermute only.
A program may use at most 64 MiB of HBM per device.

v0:
```python
import jax
import jax.numpy as jnp
from jax import lax
from jax.sharding import PartitionSpec as P

beta_first = 0.9
beta_second = 0.95
learn_rate = 0.05
weight_decay = 0.1
epsilon = 1e-08
correct_first = 1.0 - 0.9**10
correct_second = 1.0 - 0.95**10


def gram_of(rows_block):
    return jnp.dot(
        rows_block.T,
        rows_block,
        precision=lax.Precision.HIGHEST,
        preferred_element_type=jnp.float32,
    )


def left_contract(merged, other):
    return lax.dot_general(
        merged,
        other,
        (((0,), (0,)), ((), ())),
        precision=lax.Precision.HIGHEST,
        preferred_element_type=jnp.float32,
    )


def shards(grads, errors, q_prev, weight, first_moment, second_moment):
    merged = grads[0].astype(jnp.float32) + errors[0].astype(jnp.float32)
    local_factor = jnp.dot(
        merged, q_prev, precision=lax.Precision.HIGHEST, preferred_element_type=jnp.float32
    )
    factor = lax.psum(local_factor, "rep")
    gram_matrix = lax.psum(gram_of(factor), "fsdp")
    triangle = jnp.linalg.cholesky(gram_matrix)
    ortho_basis = lax.linalg.triangular_solve(
        triangle, factor, left_side=False, lower=True, transpose_a=True
    )
    local_right = left_contract(merged, ortho_basis)
    q_next = lax.psum(local_right, ("fsdp", "rep")) / lax.axis_size("rep")
    approx = jnp.dot(
        ortho_basis, q_next.T, precision=lax.Precision.HIGHEST, preferred_element_type=jnp.float32
    )
    new_errors = (merged - approx).astype(jnp.bfloat16)[None]
    first_f = beta_first * first_moment.astype(jnp.float32) + (1.0 - beta_first) * approx
    second_f = (
        beta_second * second_moment.astype(jnp.float32) + (1.0 - beta_second) * approx * approx
    )
    adam_ratio = first_f / correct_first / (jnp.sqrt(second_f / correct_second) + epsilon)
    new_weight = weight - learn_rate * (adam_ratio + weight_decay * weight)
    return (
        new_errors,
        q_next,
        new_weight,
        first_f.astype(jnp.bfloat16),
        second_f.astype(jnp.bfloat16),
    )


def solution(mesh):
    return jax.shard_map(
        shards,
        mesh=mesh,
        in_specs=(
            P("rep", "fsdp", None),
            P("rep", "fsdp", None),
            P(),
            P("fsdp", None),
            P("fsdp", None),
            P("fsdp", None),
        ),
        out_specs=(P("rep", "fsdp", None), P(), P("fsdp", None), P("fsdp", None), P("fsdp", None)),
        check_vma=False,
    )
```

profile of v0, /device:TPU:1, one launch (start us, length us, event | category | flops | bytes accessed | tf_op | source)
XLA Modules:
  0.0 429.2 jit_solution(6446979599652089542)
XLA Ops:
  7.2 0.0 copy-start
  7.2 0.0 copy-start.1
  7.2 0.0 copy-start.2
  7.2 0.0 all-reduce.3.cloned.1.call-start
  7.2 0.8 copy-done
  8.1 4.6 %fusion.3 = f32[1024,64]{0,1:T(8,128)} fusion(f32[512,64]{0,1:T(8,128)S(1)} %copy-done, bf16[1,1024,512]{2,1,0:T(8,128)(2,1)} %param.7, bf16[1,1024,512]{2,1,0:T(8,128)(2,1)} %param.6), kind=kOutput, calls=%fused_computation.5 | convolution fusion | flops 404226048 | bytes 2490368 | tf_op jit(solution)/shard_map/dot_general | solution.py:36
  12.6 0.0 all-reduce.3.cloned.1.call-update
  12.7 0.0 all-reduce.5.cloned.1.call-start
  12.7 115.2 %all-reduce.3.cloned.1.call-done = f32[1024,64]{0,1:T(8,128)} async-done(((f32[1024,64]{0,1:T(8,128)}), f32[1024,64]{0,1:T(8,128)}) %all-reduce.3.cloned.1.call-update) | async-done | bytes 262160 | tf_op jit(solution)/shard_map/psum | solution.py:39
  128.0 1.4 fusion.13
  129.3 23.0 %psum.22 = f32[64,64]{0,1:T(8,128)S(1)} all-reduce(f32[64,64]{0,1:T(8,128)S(1)} %fusion.13), channel_id=1, replica_groups=mesh['fsdp'=8,'rep'=32] {'fsdp'}, use_global_device_ids=true, to_apply=%region_1.0 | all-reduce | flops 4096 | bytes 32768 | tf_op jit(solution)/shard_map/psum | solution.py:40
  152.3 0.1 copy.12
  152.4 5.8 %cholesky.16 = f32[64,64]{1,0:T(8,128)S(1)} custom-call(f32[64,64]{1,0:T(8,128)S(1)} %fusion.12), custom_call_target="Cholesky" | custom-call | tf_op jit(solution)/shard_map/jit(cholesky)/cholesky | solution.py:41
  158.3 0.6 compare_reduce_fusion
  159.0 0.7 fusion.9
  159.6 4.9 %custom-call.6 = f32[1,64,64]{1,2,0:T(8,128)S(1)} custom-call(f32[1,64,64]{2,1,0:T(8,128)S(1)} %fusion.9), custom_call_target="InvertDiagBlocksLowerTriangular" | custom-call | tf_op jit(solution)/shard_map/triangular_solve | solution.py:42
  164.5 1.4 fusion.10
  165.9 0.0 copy-done.1
  165.9 0.0 copy-done.2
  165.9 2.3 fusion.1
  168.2 0.0 all-reduce.5.cloned.1.call-update
  168.2 244.8 %all-reduce.5.cloned.1.call-done = f32[512,64]{0,1:T(8,128)} async-done(((f32[512,64]{0,1:T(8,128)}), f32[512,64]{0,1:T(8,128)}) %all-reduce.5.cloned.1.call-update) | async-done | bytes 131088 | tf_op jit(solution)/shard_map/psum | solution.py:46
  413.1 0.9 broadcast_multiply_fusion
  414.0 0.0 copy-start.3
  414.0 8.4 %fusion.7 = (bf16[1024,512]{1,0:T(8,128)(2,1)}, f32[1024,512]{1,0:T(8,128)}, bf16[1024,512]{1,0:T(8,128)(2,1)}, bf16[1,1024,512]{2,1,0:T(8,128)(2,1)}) fusion(bf16[1024,512]{1,0:T(8,128)(2,1)} %param.11, f32[1024,512]{1,0:T(8,128)} %param.9, bf16[1024,512]{1,0:T(8,128)(2,1)} %param.10, bf16[1,1024,512]{2,1,0:T(8,128)(2,1)S(1)} %copy-done.1, ...), kind=kOutput, calls=%fused_computation.12 | convolution fusion | flops 415236096 | bytes 11927552 | tf_op jit(solution)/shard_map/dot_general | solution.py:47
  422.4 0.0 copy-done.3
  (2 shorter events, 0.0 us)
Async XLA Ops:
  7.2 0.9 copy-start
  7.2 158.7 %copy-start.1 = (bf16[1,1024,512]{2,1,0:T(8,128)(2,1)S(1)}, bf16[1,1024,512]{2,1,0:T(8,128)(2,1)}, u32[]{:S(2)}) copy-start(bf16[1,1024,512]{2,1,0:T(8,128)(2,1)} %param.7) | copy-start | bytes 3145732
  7.2 158.7 %copy-start.2 = (bf16[1,1024,512]{2,1,0:T(8,128)(2,1)S(1)}, bf16[1,1024,512]{2,1,0:T(8,128)(2,1)}, u32[]{:S(2)}) copy-start(bf16[1,1024,512]{2,1,0:T(8,128)(2,1)} %param.6) | copy-start | bytes 3145732
  7.2 120.8 %all-reduce.3.cloned.1.call-start = ((), (), s32[]{:S(2)}) async-start(), calls=%async_computation | async-start | bytes 524288 | tf_op jit(solution)/shard_map/psum | solution.py:39
  12.7 400.4 %all-reduce.5.cloned.1.call-start = ((), (), s32[]{:S(2)}) async-start(), calls=%async_computation.1 | async-start | bytes 262144 | tf_op jit(solution)/shard_map/psum | solution.py:46
  414.0 8.4 %copy-start.3 = (f32[512,64]{0,1:T(8,128)}, f32[512,64]{0,1:T(8,128)S(1)}, u32[]{:S(2)}) copy-start(f32[512,64]{0,1:T(8,128)S(1)} %broadcast_multiply_fusion) | copy-start | bytes 393220
Sparse Core Ops, SparseCore 0:
  12.8 115.1 all-reduce.2
  168.4 244.6 all-reduce.4
where the time goes:
time: 430 us; the launch traced here: 429 us
  waiting for transfers between devices  360 us (84%)
  blocking collectives  23 us (5%)
  matrix products  18 us (4%)
  between operations  14.1 us (3%)
  other arithmetic  13 us (3%)
    psum x1, waiting for transfers between devices, shards(): q_next = lax.psum(local_right, ('fsdp', 'rep')) / lax.axis_size('rep')  245 us
    psum x1, waiting for transfers between devices, shards(): factor = lax.psum(local_factor, 'rep')  115 us
    psum x1, blocking collectives, shards(): gram_matrix = lax.psum(gram_of(factor), 'fsdp')  23 us
  transfers between devices with their start and end apart: 2, of which 2 were waited for; matrix products, arithmetic and copies ran while one was open for 0% of the time, Pallas kernels for 0%

commit v1 on v0

v1 whole, which is shorter than its diff:
```python
import functools

import jax
import jax.numpy as jnp
from jax import lax
from jax.experimental import pallas as pl
from jax.experimental.pallas import tpu as pltpu
from jax.sharding import PartitionSpec as P

beta_first = 0.9
beta_second = 0.95
learn_rate = 0.05
weight_decay = 0.1
epsilon = 1e-08
correct_first = 1.0 - 0.9**10
correct_second = 1.0 - 0.95**10

ROWS, COLS, RANK, N_REP, N_FSDP = 1024, 512, 64, 32, 8
LANES = 128
f32, bf16 = jnp.float32, jnp.bfloat16
NT = (((1,), (1,)), ((), ()))
NN = (((1,), (0,)), ((), ()))
TN = (((0,), (0,)), ((), ()))


def mm(a, b, dims):
    return lax.dot_general(a, b, dims, preferred_element_type=f32)


def split3(x):
    hi = x.astype(bf16)
    rest = x - hi.astype(f32)
    mid = rest.astype(bf16)
    lo = (rest - mid.astype(f32)).astype(bf16)
    return hi, mid, lo


def stack3(x):
    return jnp.concatenate(split3(x), axis=0)


def fold3(x):
    n = x.shape[0] // 3
    return x[:n] + x[n : 2 * n] + x[2 * n :]


def exact(a, b, dims):
    a1, a2, a3 = split3(a)
    b1, b2, b3 = split3(b)
    small = mm(a1, b3, dims) + mm(a3, b1, dims) + mm(a2, b2, dims)
    return small + (mm(a1, b2, dims) + mm(a2, b1, dims)) + mm(a1, b1, dims)


LEFT_STEP = 256


def left_body(grads, errors, q_prev, out, q_parts):
    @pl.when(pl.program_id(0) == 0)
    def _():
        q_parts[...] = stack3(q_prev[...])

    q = q_parts[...]
    block = fold3(mm(q, grads[0], NT) + mm(q, errors[0], NT))
    for k in range(LEFT_STEP // LANES):
        out[k] = block[:, k * LANES : (k + 1) * LANES]


def left_factor(grads, errors, q_prev):
    steps = ROWS // LEFT_STEP
    rows = pl.BlockSpec((1, LEFT_STEP, COLS), lambda i: (0, i, 0))
    return pl.pallas_call(
        left_body,
        grid=(steps,),
        in_specs=[rows, rows, pl.BlockSpec((RANK, COLS), lambda i: (0, 0))],
        out_specs=pl.BlockSpec((LEFT_STEP // LANES, RANK, LANES), lambda i: (i, 0, 0)),
        out_shape=jax.ShapeDtypeStruct((ROWS // LANES, RANK, LANES), f32),
        scratch_shapes=[pltpu.VMEM((3 * RANK, COLS), bf16)],
        name="left_factor",
    )(grads, errors, q_prev.T)


def sum_copies_body(copies, pieces, out):
    total = pieces[0]
    for k in range(1, pieces.shape[0]):
        total = total + pieces[k]
    for k in range(copies):
        out[k] = total


def sum_copies(pieces, copies):
    return pl.pallas_call(
        functools.partial(sum_copies_body, copies),
        out_shape=jax.ShapeDtypeStruct((copies, *pieces.shape[1:]), f32),
        name="sum_copies",
    )(pieces)


def right_body(grads, errors, factor, out, acc, gram):
    step = pl.program_id(0)
    parts = stack3(jnp.concatenate([factor[k] for k in range(factor.shape[0])], axis=1))
    right = fold3(mm(parts, grads[0], NN) + mm(parts, errors[0], NN))
    square = fold3(mm(parts, parts, NT))
    square = square[:, :RANK] + square[:, RANK : 2 * RANK] + square[:, 2 * RANK :]

    @pl.when(step == 0)
    def _():
        acc[...] = right
        gram[...] = square

    @pl.when(step > 0)
    def _():
        acc[...] += right
        gram[...] += square

    @pl.when(step == pl.num_programs(0) - 1)
    def _():
        for c in range(N_REP):
            i, j = divmod(c, COLS // LANES)
            out[c, :8] = acc[8 * i : 8 * i + 8, LANES * j : LANES * (j + 1)]
            out[c, 8:] = jnp.zeros((8, LANES), f32)
        for c in range(RANK // 8):
            out[c, 8:, :RANK] = gram[8 * c : 8 * c + 8, :] * (1.0 / N_REP)


def right_term(grads, errors, factor):
    steps = 4
    n = ROWS // steps
    rows = pl.BlockSpec((1, n, COLS), lambda i: (0, i, 0))
    return pl.pallas_call(
        right_body,
        grid=(steps,),
        in_specs=[rows, rows, pl.BlockSpec((n // LANES, RANK, LANES), lambda i: (i, 0, 0))],
        out_specs=pl.BlockSpec((N_REP, 16, LANES), lambda i: (0, 0, 0)),
        out_shape=jax.ShapeDtypeStruct((N_REP, 16, LANES), f32),
        scratch_shapes=[pltpu.VMEM((RANK, COLS), f32), pltpu.VMEM((RANK, RANK), f32)],
        name="right_term",
    )(grads, errors, factor)


def inverse_triangle(gram):
    eye = (
        lax.broadcasted_iota(jnp.int32, (RANK, RANK), 0)
        == lax.broadcasted_iota(jnp.int32, (RANK, RANK), 1)
    ).astype(f32)
    both = jnp.concatenate([gram, eye], axis=1)
    below = lax.broadcasted_iota(jnp.int32, (RANK, 1), 0)
    roots = jnp.zeros((RANK, 1), f32)
    for k in range(RANK):
        pivot_row = both[k : k + 1, :]
        column = both[:, k : k + 1]
        pivot = pivot_row[:, k : k + 1]
        roots = jnp.where(below == k, lax.rsqrt(pivot), roots)
        scale = jnp.where(below > k, column / pivot, 0.0)
        both = both - scale * pivot_row
    return both[:, RANK:] * roots


def final_body(
    grads, errors, factor, sums, weight, first, second,
    new_errors, q_next, new_weight, new_first, new_second, mix,
):
    @pl.when(pl.program_id(0) == 0)
    def _():
        gram = jnp.concatenate([sums[c, 8:, :RANK] for c in range(RANK // 8)], axis=0)
        wide = COLS // LANES
        right = jnp.concatenate(
            [
                jnp.concatenate([sums[i * wide + j, :8] for j in range(wide)], axis=1)
                for i in range(RANK // 8)
            ],
            axis=0,
        )
        inverse = inverse_triangle(gram)
        q_t = exact(inverse, right, NN) * (1.0 / N_REP)
        q_next[...] = q_t
        w1, w2, w3 = split3(exact(inverse, q_t, TN))
        mix[...] = jnp.concatenate([w1, w2, w1, w3, w2, w1], axis=0)

    f1, f2, f3 = split3(factor[0])
    approx = mm(jnp.concatenate([f1, f1, f2, f1, f2, f3], axis=0), mix[...], TN)
    merged = grads[0].astype(f32) + errors[0].astype(f32)
    new_errors[0] = (merged - approx).astype(bf16)
    first_f = beta_first * first[...].astype(f32) + (1.0 - beta_first) * approx
    second_f = beta_second * second[...].astype(f32) + (1.0 - beta_second) * approx * approx
    ratio = first_f / correct_first / (jnp.sqrt(second_f / correct_second) + epsilon)
    w = weight[...]
    new_weight[...] = w - learn_rate * (ratio + weight_decay * w)
    new_first[...] = first_f.astype(bf16)
    new_second[...] = second_f.astype(bf16)


def final(grads, errors, factor, sums, weight, first, second):
    n = LANES
    rows3 = pl.BlockSpec((1, n, COLS), lambda i: (0, i, 0))
    rows2 = pl.BlockSpec((n, COLS), lambda i: (i, 0))
    return pl.pallas_call(
        final_body,
        grid=(ROWS // n,),
        in_specs=[
            rows3, rows3,
            pl.BlockSpec((1, RANK, LANES), lambda i: (i, 0, 0)),
            pl.BlockSpec((N_REP, 16, LANES), lambda i: (0, 0, 0)),
            rows2, rows2, rows2,
        ],
        out_specs=[rows3, pl.BlockSpec((RANK, COLS), lambda i: (0, 0)), rows2, rows2, rows2],
        out_shape=[
            jax.ShapeDtypeStruct((1, ROWS, COLS), bf16),
            jax.ShapeDtypeStruct((RANK, COLS), f32),
            jax.ShapeDtypeStruct((ROWS, COLS), f32),
            jax.ShapeDtypeStruct((ROWS, COLS), bf16),
            jax.ShapeDtypeStruct((ROWS, COLS), bf16),
        ],
        scratch_shapes=[pltpu.VMEM((6 * RANK, COLS), bf16)],
        name="final",
    )(grads, errors, factor, sums, weight, first, second)


def exchange(x, axis):
    return lax.all_to_all(x, axis, 0, 0)


def shards(grads, errors, q_prev, weight, first_moment, second_moment):
    local = left_factor(grads, errors, q_prev).reshape(N_REP, 16, LANES)
    factor = exchange(sum_copies(exchange(local, "rep"), N_REP), "rep")
    factor = factor.reshape(ROWS // LANES, RANK, LANES)
    right = exchange(right_term(grads, errors, factor), "rep")
    right = exchange(sum_copies(right, N_FSDP), "fsdp")
    sums = exchange(sum_copies(right, N_REP), "rep")
    outs = final(grads, errors, factor, sums, weight, first_moment, second_moment)
    return outs[0], outs[1].T, *outs[2:]


def solution(mesh):
    return jax.shard_map(
        shards,
        mesh=mesh,
        in_specs=(
            P("rep", "fsdp", None),
            P("rep", "fsdp", None),
            P(),
            P("fsdp", None),
            P("fsdp", None),
            P("fsdp", None),
        ),
        out_specs=(P("rep", "fsdp", None), P(), P("fsdp", None), P("fsdp", None), P("fsdp", None)),
        check_vma=False,
    )
```

time: 430 us -> 105 us (0.24)
  waiting for transfers between devices: 360 us -> 0 us
  blocking collectives: 23 us -> 75.1 us
  Pallas kernels: 0 us -> 28.2 us
  matrix products: 18 us -> 0 us
  between operations: 14.1 us -> 0.64 us
  other arithmetic: 13 us -> 0 us
    psum x2 -> x0, waiting for transfers between devices: 360 us -> none  [the longest x1 245 us: shards(): q_next = lax.psum(local_right, ('fsdp', 'rep')) / lax.axis_size('rep')]
    all_to_all x0 -> x5, blocking collectives: none -> 75.1 us  [exchange(): return lax.all_to_all(x, axis, 0, 0)]
    pallas_call x0 -> x6, Pallas kernels: none -> 28.2 us  [the longest x1 15.3 us: final(): pl.pallas_call(final_body, grid=(ROWS // n,), in_specs=[rows3, rows3, pl....]
    psum x1 -> x0, blocking collectives: 23 us -> none  [shards(): gram_matrix = lax.psum(gram_of(factor), 'fsdp')]
    dot_general x4 -> x0, matrix products: 16.6 us -> none  [the longest x1 8.38 us: shards(): jnp.dot(ortho_basis, q_next.T, precision=lax.Precision.HIGHEST, preferred...]
    another operation x5 -> x0, other arithmetic: 12.1 us -> none  [the longest x3 6.52 us: shards(): triangle = jnp.linalg.cholesky(gram_matrix)]
  transfers between devices with their start and end apart: 2 -> 0, of which waited for: 2 -> 0; matrix products, arithmetic and copies ran while one was open for 0% -> 0% of each run, Pallas kernels for 0% -> 0%
where the time goes in v1:
time: 105 us; the launch traced here: 104 us
  blocking collectives  75.1 us (72%)
  Pallas kernels  28.2 us (27%)
    all_to_all x5, blocking collectives, exchange(): return lax.all_to_all(x, axis, 0, 0)  75.1 us
    pallas_call x1, Pallas kernels, final(): pl.pallas_call(final_body, grid=(ROWS // n,), in_specs=[rows3, rows3, pl....  15.3 us
    pallas_call x3, Pallas kernels, sum_copies(): pl.pallas_call(functools.partial(sum_copies_body, copies), out_shape=jax....  4.88 us
    pallas_call x1, Pallas kernels, left_factor(): pl.pallas_call(left_body, grid=(steps,), in_specs=[rows, rows, pl.BlockSp...  4.09 us
    pallas_call x1, Pallas kernels, right_term(): pl.pallas_call(right_body, grid=(steps,), in_specs=[rows, rows, pl.BlockS...  3.97 us

profile of v1, /device:TPU:1, one launch (start us, length us, event | category | flops | bytes accessed | tf_op | source)
XLA Modules:
  0.0 104.0 jit_solution(16146172759545560243)
XLA Ops:
  0.6 4.1 %left_factor.1 = f32[8,64,128]{2,1,0:T(8,128)} custom-call(bf16[1,1024,512]{2,1,0:T(8,128)(2,1)} %grads.5, bf16[1,1024,512]{2,1,0:T(8,128)(2,1)} %errors.5, f32[64,512]{1,0:T(8,128)} %bitcast.7), custom_call_target="tpu_custom_call" | custom-call | tf_op jit(solution)/shard_map/left_factor/pallas_call | solution.py:71
  4.7 17.7 %all_to_all.25.pieces = f32[32,16,128]{2,1,0:T(8,128)} all-to-all(f32[32,16,128]{2,1,0:T(8,128)} %bitcast.6), channel_id=1, replica_groups=mesh['fsdp'=8,'rep'=32] {'rep'}, dimensions={0} | all-to-all | bytes 524288 | tf_op jit(solution)/shard_map/all_to_all | solution.py:219
  22.4 1.7 %sum_copies.3 = f32[32,16,128]{2,1,0:T(8,128)} custom-call(f32[32,16,128]{2,1,0:T(8,128)} %all_to_all.25.pieces), custom_call_target="tpu_custom_call" | custom-call | tf_op jit(solution)/shard_map/sum_copies/pallas_call | solution.py:91
  24.1 13.5 %all_to_all.26 = f32[32,16,128]{2,1,0:T(8,128)} all-to-all(f32[32,16,128]{2,1,0:T(8,128)} %sum_copies.3), channel_id=1, replica_groups=mesh['fsdp'=8,'rep'=32] {'rep'}, dimensions={0} | all-to-all | bytes 524288 | tf_op jit(solution)/shard_map/all_to_all | solution.py:219
  37.6 4.0 %right_term.1 = f32[32,16,128]{2,1,0:T(8,128)} custom-call(bf16[1,1024,512]{2,1,0:T(8,128)(2,1)} %grads.5, bf16[1,1024,512]{2,1,0:T(8,128)(2,1)} %errors.5, f32[8,64,128]{2,1,0:T(8,128)} %bitcast.4), custom_call_target="tpu_custom_call" | custom-call | tf_op jit(solution)/shard_map/right_term/pallas_call | solution.py:129
  41.6 13.5 %all_to_all.27.pieces = f32[32,16,128]{2,1,0:T(8,128)} all-to-all(f32[32,16,128]{2,1,0:T(8,128)} %right_term.1), channel_id=1, replica_groups=mesh['fsdp'=8,'rep'=32] {'rep'}, dimensions={0} | all-to-all | bytes 524288 | tf_op jit(solution)/shard_map/all_to_all | solution.py:219
  55.1 1.6 %sum_copies.4 = f32[8,16,128]{2,1,0:T(8,128)} custom-call(f32[32,16,128]{2,1,0:T(8,128)} %all_to_all.27.pieces), custom_call_target="tpu_custom_call" | custom-call | tf_op jit(solution)/shard_map/sum_copies/pallas_call | solution.py:91
  56.7 15.5 %all_to_all.28.pieces = f32[8,16,128]{2,1,0:T(8,128)} all-to-all(f32[8,16,128]{2,1,0:T(8,128)} %sum_copies.4), channel_id=1, replica_groups=mesh['fsdp'=8,'rep'=32] {'fsdp'}, dimensions={0} | all-to-all | bytes 131072 | tf_op jit(solution)/shard_map/all_to_all | solution.py:219
  72.1 1.6 %sum_copies.5 = f32[32,16,128]{2,1,0:T(8,128)} custom-call(f32[8,16,128]{2,1,0:T(8,128)} %all_to_all.28.pieces), custom_call_target="tpu_custom_call" | custom-call | tf_op jit(solution)/shard_map/sum_copies/pallas_call | solution.py:91
  73.7 15.0 %all_to_all.29.sums = f32[32,16,128]{2,1,0:T(8,128)} all-to-all(f32[32,16,128]{2,1,0:T(8,128)} %sum_copies.5), channel_id=1, replica_groups=mesh['fsdp'=8,'rep'=32] {'rep'}, dimensions={0} | all-to-all | bytes 524288 | tf_op jit(solution)/shard_map/all_to_all | solution.py:219
  88.7 15.3 %final.1 = (bf16[1,1024,512]{2,1,0:T(8,128)(2,1)}, f32[64,512]{1,0:T(8,128)}, f32[1024,512]{1,0:T(8,128)}, bf16[1024,512]{1,0:T(8,128)(2,1)}, bf16[1024,512]{1,0:T(8,128)(2,1)}) custom-call(bf16[1,1024,512]{2,1,0:T(8,128)(2,1)} %grads.5, bf16[1,1024,512]{2,1,0:T(8,128)(2,1)} %errors.5, f32[8,64,128]{2,1,0:T(8,128)} %bitcast.5, ...), custom_call_target="tpu_custom_call" | custom-call | tf_op jit(solution)/shard_map/final/pallas_call | solution.py:196

commit v2 on v0

v2 whole, which is shorter than its diff:
```python
import functools

import jax
import jax.numpy as jnp
from jax import lax
from jax.experimental import pallas as pl
from jax.experimental.pallas import tpu as pltpu
from jax.sharding import PartitionSpec as P

beta_first = 0.9
beta_second = 0.95
learn_rate = 0.05
weight_decay = 0.1
epsilon = 1e-08
correct_first = 1.0 - 0.9**10
correct_second = 1.0 - 0.95**10

ROWS, COLS, RANK, N_REP, N_FSDP = 1024, 512, 64, 32, 8
HALF, N_CHIP, PIECE = ROWS // 2, N_REP // 2, 16
LANES = 128
f32, bf16 = jnp.float32, jnp.bfloat16
NT = (((1,), (1,)), ((), ()))
NN = (((1,), (0,)), ((), ()))
TN = (((0,), (0,)), ((), ()))


def mm(a, b, dims):
    return lax.dot_general(a, b, dims, preferred_element_type=f32)


def split3(x):
    hi = x.astype(bf16)
    rest = x - hi.astype(f32)
    mid = rest.astype(bf16)
    lo = (rest - mid.astype(f32)).astype(bf16)
    return hi, mid, lo


def stack3(x):
    return jnp.concatenate(split3(x), axis=0)


def fold3(x):
    n = x.shape[0] // 3
    return x[:n] + x[n : 2 * n] + x[2 * n :]


def exact(a, b, dims):
    a1, a2, a3 = split3(a)
    b1, b2, b3 = split3(b)
    small = mm(a1, b3, dims) + mm(a3, b1, dims) + mm(a2, b2, dims)
    return small + (mm(a1, b2, dims) + mm(a2, b1, dims)) + mm(a1, b1, dims)


SMEM = pl.BlockSpec(memory_space=pltpu.SMEM)
VMEM = pl.BlockSpec(memory_space=pltpu.VMEM)
ANY = pl.BlockSpec(memory_space=pl.ANY)


def call(body, name, ins, outs, limit, scratch=(), cost=0):
    return pl.pallas_call(
        body,
        in_specs=ins,
        out_specs=[VMEM if m is None else m for _, _, m in outs],
        out_shape=[
            pltpu.VMEM(s, t) if m is None else jax.ShapeDtypeStruct(s, t) for s, t, m in outs
        ],
        scratch_shapes=scratch,
        compiler_params=pltpu.CompilerParams(vmem_limit_bytes=limit << 20),
        cost_estimate=pl.CostEstimate(flops=cost, bytes_accessed=cost // 64, transcendentals=0),
        name=name,
    )


def tile_columns(block, out):
    for k in range(out.shape[0]):
        out[k] = block[:, k * LANES : (k + 1) * LANES]


def left_first_body(core, grads, errors, q_prev, other, g_all, e_all, q_parts, q_buf, sems, q_sem):
    mine, theirs = core[0], 1 - core[0]
    q_copy = pltpu.make_async_copy(q_prev, q_buf, q_sem)
    copies = []
    for n, half in enumerate((theirs, mine)):
        rows = pl.ds(pl.multiple_of(half * HALF, HALF), HALF)
        copies.append(pltpu.make_async_copy(grads.at[0, rows], g_all.at[rows], sems.at[2 * n]))
        copies.append(pltpu.make_async_copy(errors.at[0, rows], e_all.at[rows], sems.at[2 * n + 1]))
    copies[0].start()
    copies[1].start()
    q_copy.start()
    copies[2].start()
    copies[3].start()
    q_copy.wait()
    q_parts[...] = stack3(q_buf[...])
    copies[0].wait()
    copies[1].wait()
    rows = pl.ds(pl.multiple_of(theirs * HALF, HALF), HALF)
    tile_columns(fold3(mm(q_parts[...], g_all[rows], NT) + mm(q_parts[...], e_all[rows], NT)), other)
    copies[2].wait()
    copies[3].wait()


def in_hbm(x):
    return pltpu.with_memory_space_constraint(x, pltpu.HBM)


def left_first(core, grads, errors, q_prev):
    return call(
        left_first_body, "left_first", [SMEM, ANY, ANY, ANY],
        [
            ((HALF // LANES, RANK, LANES), f32, None),
            ((ROWS, COLS), bf16, None),
            ((ROWS, COLS), bf16, None),
            ((3 * RANK, COLS), bf16, None),
        ],
        16,
        [pltpu.VMEM((RANK, COLS), f32), pltpu.SemaphoreType.DMA((4,)), pltpu.SemaphoreType.DMA],
        cost=200_000_000,
    )(core, in_hbm(grads), in_hbm(errors), in_hbm(q_prev.T))


def left_own_body(core, g_all, e_all, q_parts, out):
    rows = pl.ds(pl.multiple_of(core[0] * HALF, HALF), HALF)
    tile_columns(fold3(mm(q_parts[...], g_all[rows], NT) + mm(q_parts[...], e_all[rows], NT)), out)


def left_own(core, g_all, e_all, q_parts):
    return call(
        left_own_body, "left_own", [SMEM, VMEM, VMEM, VMEM],
        [((HALF // LANES, RANK, LANES), f32, None)], 8, cost=200_000_000,
    )(core, g_all, e_all, q_parts)[0]


def add_body(a, b, out):
    out[...] = a[...] + b[...]


def add(a, b):
    return call(add_body, "add", [VMEM, VMEM], [(a.shape, f32, None)], 4)(a, b)[0]


def sum_copies_body(pieces, out):
    total = pieces[0]
    for k in range(1, pieces.shape[0]):
        total = total + pieces[k]
    for k in range(out.shape[0]):
        out[k] = total


def sum_copies(pieces, copies):
    shape = (copies, *pieces.shape[1:])
    return call(sum_copies_body, "sum_copies", [VMEM], [(shape, f32, None)], 4)(pieces)[0]


def factor_parts(factor):
    return stack3(jnp.concatenate([factor[k] for k in range(factor.shape[0])], axis=1))


def square_of(parts):
    square = fold3(mm(parts, parts, NT))
    return square[:, :RANK] + square[:, RANK : 2 * RANK] + square[:, 2 * RANK :]


def right_first_body(core, g_all, e_all, factor, right, gram):
    rows = pl.ds(pl.multiple_of(core[0] * HALF, HALF), HALF)
    parts = factor_parts(factor)
    right[...] = fold3(mm(parts, g_all[rows], NN) + mm(parts, e_all[rows], NN))
    gram[...] = square_of(parts)


def right_first(core, g_all, e_all, factor):
    return call(
        right_first_body, "right_first", [SMEM, VMEM, VMEM, VMEM],
        [((RANK, COLS), f32, None), ((RANK, RANK), f32, None)], 8, cost=200_000_000,
    )(core, g_all, e_all, factor)


def half_tiles(block, out):
    for c in range(N_CHIP):
        i, j = divmod(c, COLS // 2 // LANES)
        out[c, :8] = block[8 * i : 8 * i + 8, LANES * j : LANES * (j + 1)]


def right_half(core, flip, g_all, e_all, parts, first):
    rows = pl.ds(pl.multiple_of((1 - core[0]) * HALF, HALF), HALF)
    half = core[0] if not flip else 1 - core[0]
    columns = pl.ds(pl.multiple_of(half * (COLS // 2), COLS // 2), COLS // 2)
    block = fold3(mm(parts, g_all[rows, columns], NN) + mm(parts, e_all[rows, columns], NN))
    return first[:, columns] + block


def right_theirs_body(core, g_all, e_all, factor, first, out):
    block = right_half(core, True, g_all, e_all, factor_parts(factor), first)
    for c in range(N_CHIP):
        i, j = divmod(c, COLS // 2 // LANES)
        out[c] = block[8 * i : 8 * i + 8, LANES * j : LANES * (j + 1)]


def right_theirs(core, g_all, e_all, factor, first):
    return call(
        right_theirs_body, "right_theirs", [SMEM, VMEM, VMEM, VMEM, VMEM],
        [((N_CHIP, 8, LANES), f32, None)], 8, cost=100_000_000,
    )(core, g_all, e_all, factor, first)[0]


def right_own_body(core, g_all, e_all, factor, first, gram, out):
    parts = factor_parts(factor)
    block = right_half(core, False, g_all, e_all, parts, first)
    square = (gram[...] + square_of(parts)) * (1.0 / N_CHIP)
    for c in range(N_CHIP):
        i, j = divmod(c, COLS // 2 // LANES)
        out[c, :8] = block[8 * i : 8 * i + 8, LANES * j : LANES * (j + 1)]
        out[c, 8:] = jnp.zeros((8, LANES), f32)
    for c in range(RANK // 8):
        out[c, 8:, :RANK] = square[8 * c : 8 * c + 8, :]


def right_own(core, g_all, e_all, factor, first, gram):
    return call(
        right_own_body, "right_own", [SMEM, VMEM, VMEM, VMEM, VMEM, VMEM],
        [((N_CHIP, PIECE, LANES), f32, None)], 8, cost=100_000_000,
    )(core, g_all, e_all, factor, first, gram)[0]


def right_join_body(own, arrived, out):
    out[:, :8] = own[:, :8] + arrived[...]
    out[:, 8:] = own[:, 8:]


def right_join(own, arrived):
    return call(
        right_join_body, "right_join", [VMEM, VMEM], [(own.shape, f32, None)], 4
    )(own, arrived)[0]


def inverse_triangle(gram):
    eye = (
        lax.broadcasted_iota(jnp.int32, (RANK, RANK), 0)
        == lax.broadcasted_iota(jnp.int32, (RANK, RANK), 1)
    ).astype(f32)
    both = jnp.concatenate([gram, eye], axis=1)
    groups = RANK // 8
    rows = [both[8 * g : 8 * g + 8] for g in range(groups)]
    tile = (8, 2 * RANK)
    sub = lax.broadcasted_iota(jnp.int32, tile, 0)
    done = []
    for b in range(groups):
        columns = [
            [
                jnp.broadcast_to(rows[g][:, 8 * b + j : 8 * b + j + 1], tile)
                for g in range(b, groups)
            ]
            for j in range(8)
        ]
        roots = jnp.zeros(tile, f32)
        for k in range(8):
            pivot = jnp.broadcast_to(columns[k][0][k : k + 1], tile)
            inv = 1.0 / pivot
            roots = jnp.where(sub == k, lax.rsqrt(pivot), roots)
            scale = [c * inv for c in columns[k]]
            scale[0] = jnp.where(sub > k, scale[0], 0.0)
            for j in range(k + 1, 8):
                head = jnp.broadcast_to(columns[j][0][k : k + 1], tile)
                columns[j] = [c - x * head for c, x in zip(columns[j], scale)]
            row = jnp.broadcast_to(rows[b][k : k + 1], tile)
            for g in range(b, groups):
                rows[g] = rows[g] - scale[g - b] * row
        done.append(rows[b] * roots)
    return jnp.concatenate(done, axis=0)[:, RANK:]


def solve_body(sums, inverse):
    gram = jnp.concatenate([sums[c, 8:, :RANK] for c in range(RANK // 8)], axis=0)
    inverse[...] = inverse_triangle(gram)


def solve(sums):
    return call(
        solve_body, "solve", [VMEM], [((RANK, RANK), f32, None)], 4, cost=4_000_000_000
    )(sums)[0]


STEP = 128


def final_body(
    core, grads, errors, factor_own, factor_other, sums_own, sums_other, inverse, weight, first, second,
    new_errors, q_next, new_weight, new_first, new_second,
    right, mix, factor, err_buf, weight_buf, first_buf, second_buf, sems,
):
    half = COLS // 2
    for source, place in ((sums_own, core[0]), (sums_other, 1 - core[0])):
        block = jnp.concatenate(
            [
                jnp.concatenate([source[2 * i, :8], source[2 * i + 1, :8]], axis=1)
                for i in range(RANK // 8)
            ],
            axis=0,
        )
        right[:, pl.ds(pl.multiple_of(place * half, half), half)] = block
    q_t = exact(inverse[...], right[...], NN) * (1.0 / N_REP)
    q_next[...] = q_t
    w1, w2, w3 = split3(exact(inverse[...], q_t, TN))
    mix[...] = jnp.concatenate([w1, w2, w1, w3, w2, w1], axis=0)
    tiles = HALF // LANES
    factor[pl.ds(core[0] * tiles, tiles)] = factor_own[...]
    factor[pl.ds((1 - core[0]) * tiles, tiles)] = factor_other[...]

    copies = []
    for step in range(ROWS // STEP):
        rows = pl.ds(step * STEP, STEP)
        per = STEP // LANES
        piece = jnp.concatenate([factor[step * per + k] for k in range(per)], axis=1)
        f1, f2, f3 = split3(piece)
        approx = mm(jnp.concatenate([f1, f1, f2, f1, f2, f3], axis=0), mix[...], TN)
        merged = grads[rows].astype(f32) + errors[rows].astype(f32)
        err_buf[rows] = (merged - approx).astype(bf16)
        first_f = beta_first * first[rows].astype(f32) + (1.0 - beta_first) * approx
        second_f = beta_second * second[rows].astype(f32) + ((1.0 - beta_second) * approx) * approx
        first_buf[rows] = first_f.astype(bf16)
        second_buf[rows] = second_f.astype(bf16)
        root = second_f * lax.rsqrt(second_f) * (1.0 / correct_second) ** 0.5 + epsilon
        ratio = (first_f * (learn_rate / correct_first)) / root
        weight_buf[rows] = weight[rows] * (1.0 - learn_rate * weight_decay) - ratio
        for n, (buf, out) in enumerate(
            (
                (err_buf, new_errors.at[0]),
                (weight_buf, new_weight),
                (first_buf, new_first),
                (second_buf, new_second),
            )
        ):
            copy = pltpu.make_async_copy(buf.at[rows], out.at[rows], sems.at[n, step])
            copy.start()
            copies.append(copy)
    for copy in copies:
        copy.wait()


def final(core, grads, errors, factor_own, factor_other, sums_own, sums_other, inverse, weight, first, second):
    wide = (ROWS, COLS)
    return call(
        final_body, "final", [SMEM] + [VMEM] * 10,
        [
            ((1, *wide), bf16, ANY),
            ((RANK, COLS), f32, VMEM),
            (wide, f32, ANY),
            (wide, bf16, ANY),
            (wide, bf16, ANY),
        ],
        16,
        [
            pltpu.VMEM((RANK, COLS), f32),
            pltpu.VMEM((6 * RANK, COLS), bf16),
            pltpu.VMEM((ROWS // LANES, RANK, LANES), f32),
            pltpu.VMEM(wide, bf16),
            pltpu.VMEM(wide, f32),
            pltpu.VMEM(wide, bf16),
            pltpu.VMEM(wide, bf16),
            pltpu.SemaphoreType.DMA((4, ROWS // STEP)),
        ],
        cost=400_000_000,
    )(core, grads, errors, factor_own, factor_other, sums_own, sums_other, inverse, weight, first, second)


PLANE = [[2 * p + c for p in range(N_CHIP)] for c in range(2)]
SWAP = [(i, i ^ 1) for i in range(N_REP)]


def exchange(x):
    return lax.all_to_all(x, "rep", 0, 0, axis_index_groups=PLANE)


def swap(x):
    return lax.ppermute(x, "rep", SWAP)


def shards(grads, errors, q_prev, weight, first_moment, second_moment):
    core = (lax.axis_index("rep") % 2).astype(jnp.int32).reshape(1)
    theirs, g_all, e_all, q_parts = left_first(core, grads, errors, q_prev)
    arrived = swap(theirs)
    own = left_own(core, g_all, e_all, q_parts)
    pieces = add(own, arrived).reshape(N_CHIP, PIECE, LANES)
    factor_own = exchange(sum_copies(exchange(pieces), N_CHIP)).reshape(own.shape)
    factor_other = swap(factor_own)
    first, gram = right_first(core, g_all, e_all, factor_own)
    arrived = swap(right_theirs(core, g_all, e_all, factor_other, first))
    own = right_own(core, g_all, e_all, factor_other, first, gram)
    pieces = sum_copies(exchange(right_join(own, arrived)), N_FSDP)
    pieces = sum_copies(lax.all_to_all(pieces, "fsdp", 0, 0), N_CHIP)
    sums_own = exchange(pieces)
    sums_other = swap(sums_own)
    inverse = solve(sums_own)
    outs = final(
        core, g_all, e_all, factor_own, factor_other, sums_own, sums_other, inverse,
        weight, first_moment, second_moment,
    )
    return outs[0], outs[1].T, *outs[2:]


def solution(mesh):
    return jax.shard_map(
        shards,
        mesh=mesh,
        in_specs=(
            P("rep", "fsdp", None),
            P("rep", "fsdp", None),
            P(),
            P("fsdp", None),
            P("fsdp", None),
            P("fsdp", None),
        ),
        out_specs=(P("rep", "fsdp", None), P(), P("fsdp", None), P("fsdp", None), P("fsdp", None)),
        check_vma=False,
    )
```

time: 430 us -> 80.2 us (0.19)
  waiting for transfers between devices: 360 us -> 1.48 us
  blocking collectives: 23 us -> 56.9 us
  matrix products: 18 us -> 0 us
  between operations: 14.1 us -> 0.72 us
  other arithmetic: 13 us -> 0 us
  starting transfers between devices: 0.08 us -> 10.9 us
  Pallas kernels: 0 us -> 9.86 us
    psum x2 -> x0, waiting for transfers between devices: 360 us -> none  [the longest x1 245 us: shards(): q_next = lax.psum(local_right, ('fsdp', 'rep')) / lax.axis_size('rep')]
    all_to_all x0 -> x5, blocking collectives: none -> 56.9 us  [the longest x4 41.7 us: exchange(): return lax.all_to_all(x, 'rep', 0, 0, axis_index_groups=PLANE)]
    psum x1 -> x0, blocking collectives: 23 us -> none  [shards(): gram_matrix = lax.psum(gram_of(factor), 'fsdp')]
    dot_general x4 -> x0, matrix products: 16.6 us -> none  [the longest x1 8.38 us: shards(): jnp.dot(ortho_basis, q_next.T, precision=lax.Precision.HIGHEST, preferred...]
    another operation x5 -> x0, other arithmetic: 12.1 us -> none  [the longest x3 6.52 us: shards(): triangle = jnp.linalg.cholesky(gram_matrix)]
    ppermute x0 -> x4, starting transfers between devices: none -> 10.9 us  [swap(): return lax.ppermute(x, 'rep', SWAP)]
    pallas_call x0 -> x12, Pallas kernels: none -> 9.86 us  [the longest x1 4.25 us: final(): call(final_body, 'final', [SMEM] + [VMEM] * 10, [((1, *wide), bf16, ANY),...]
  transfers between devices with their start and end apart: 2 -> 4, of which waited for: 2 -> 3; matrix products, arithmetic and copies ran while one was open for 0% -> 0% of each run, Pallas kernels for 0% -> 4%
where the time goes in v2:
time: 80.2 us; the launch traced here: 79.9 us
  blocking collectives  56.9 us (71%)
  starting transfers between devices  10.9 us (14%)
  Pallas kernels  9.86 us (12%)
  waiting for transfers between devices  1.48 us (2%)
    all_to_all x4, blocking collectives, exchange(): return lax.all_to_all(x, 'rep', 0, 0, axis_index_groups=PLANE)  41.7 us
    all_to_all x1, blocking collectives, shards(): pieces = sum_copies(lax.all_to_all(pieces, 'fsdp', 0, 0), N_CHIP)  15.2 us
    ppermute x4, starting transfers between devices, swap(): return lax.ppermute(x, 'rep', SWAP)  10.9 us
    pallas_call x1, Pallas kernels, final(): call(final_body, 'final', [SMEM] + [VMEM] * 10, [((1, *wide), bf16, ANY),...  4.25 us
    pallas_call x1, Pallas kernels, left_first(): call(left_first_body, 'left_first', [SMEM, ANY, ANY, ANY], [((HALF // LAN...  1.96 us
    pallas_call x1, Pallas kernels, solve(): call(solve_body, 'solve', [VMEM], [((RANK, RANK), f32, None)], 4, cost=40...  1.91 us
  transfers between devices with their start and end apart: 4, of which 3 were waited for; matrix products, arithmetic and copies ran while one was open for 0% of the time, Pallas kernels for 4%

profile of v2, /device:TPU:1, one launch (start us, length us, event | category | flops | bytes accessed | tf_op | source)
XLA Modules:
  0.0 79.9 jit_solution(1671017458505607703)
XLA Ops:
  0.6 2.0 %left_first.1 = (f32[4,64,128]{2,1,0:T(8,128)S(1)}, bf16[1024,512]{1,0:T(8,128)(2,1)S(1)}, bf16[1024,512]{1,0:T(8,128)(2,1)S(1)}, bf16[192,512]{1,0:T(8,128)(2,1)S(1)}) custom-call(s32[1]{0:T(128)} %bitcast.core, bf16[1,1024,512]{2,1,0:T(8,128)(2,1)} %grads.1, bf16[1,1024,512]{2,1,0:T(8,128)(2,1)} %errors.1, f32[64,512]{1,0:T(8,128)} %bitcast.9), custom_call_target="tpu_custom_call" | custom-call | flops 200000000 | bytes 3125000 | tf_op jit(solution)/shard_map/left_first/pallas_call | solution.py:108
  2.6 3.3 %collective-permute-start = (f32[4,64,128]{2,1,0:T(8,128)S(1)}, f32[4,64,128]{2,1,0:T(8,128)S(1)}, u32[]{:S(2)}, u32[]{:S(2)}) collective-permute-start(f32[4,64,128]{2,1,0:T(8,128)S(1)} %get-tuple-element.19), channel_id=1, source_target_pairs={{0,1},{1,0},{2,3},{3,2},{4,5},{5,4},{6,7},{7,6},{8,9},{9,8},{10,11... | collective-permute-start | bytes 393224 | tf_op jit(solution)/shard_map/ppermute | solution.py:375
  5.9 0.5 left_own.1.a
  6.4 0.5 collective-permute-done.b
  6.9 11.5 %all_to_all.25.pieces = f32[16,16,128]{2,1,0:T(8,128)S(1)} all-to-all(f32[16,16,128]{2,1,0:T(8,128)S(1)} %bitcast.8), channel_id=1, replica_groups={{0,2,4,6,8,10,12,14,16,18,20,22,24,26,28,30},{1,3,5,7,9,11,13,15,17,19,..., dimensions={0} | all-to-all | bytes 262144 | tf_op jit(solution)/shard_map/all_to_all | solution.py:371
  18.5 10.2 %all_to_all.26 = f32[16,16,128]{2,1,0:T(8,128)S(1)} all-to-all(f32[16,16,128]{2,1,0:T(8,128)S(1)} %sum_copies.3), channel_id=1, replica_groups={{0,2,4,6,8,10,12,14,16,18,20,22,24,26,28,30},{1,3,5,7,9,11,13,15,17,19,..., dimensions={0} | all-to-all | bytes 262144 | tf_op jit(solution)/shard_map/all_to_all | solution.py:371
  28.7 2.9 %collective-permute-start.1 = (f32[4,64,128]{2,1,0:T(8,128)S(1)}, f32[4,64,128]{2,1,0:T(8,128)S(1)}, u32[]{:S(2)}, u32[]{:S(2)}) collective-permute-start(f32[4,64,128]{2,1,0:T(8,128)S(1)} %bitcast.5), channel_id=1, source_target_pairs={{0,1},{1,0},{2,3},{3,2},{4,5},{5,4},{6,7},{7,6},{8,9},{9,8},{10,11... | collective-permute-start | bytes 393224 | tf_op jit(solution)/shard_map/ppermute | solution.py:375
  31.5 0.5 right_first.1
  32.0 0.5 collective-permute-done.1.factor.factor_other
  32.5 0.3 right_theirs.1
  32.8 0.5 collective-permute-start.2
  33.2 0.4 right_own.1.own
  33.6 0.5 collective-permute-done.2.arrived
  34.2 9.8 %all_to_all.27.pieces = f32[16,16,128]{2,1,0:T(8,128)S(1)} all-to-all(f32[16,16,128]{2,1,0:T(8,128)S(1)} %right_join.1), channel_id=1, replica_groups={{0,2,4,6,8,10,12,14,16,18,20,22,24,26,28,30},{1,3,5,7,9,11,13,15,17,19,..., dimensions={0} | all-to-all | bytes 262144 | tf_op jit(solution)/shard_map/all_to_all | solution.py:371
  44.0 15.2 %all_to_all.28.pieces = f32[8,16,128]{2,1,0:T(8,128)S(1)} all-to-all(f32[8,16,128]{2,1,0:T(8,128)S(1)} %sum_copies.4), channel_id=1, replica_groups=mesh['fsdp'=8,'rep'=32] {'fsdp'}, dimensions={0} | all-to-all | bytes 131072 | tf_op jit(solution)/shard_map/all_to_all | solution.py:390
  59.2 10.2 %all_to_all.29.sums.sums_own = f32[16,16,128]{2,1,0:T(8,128)S(1)} all-to-all(f32[16,16,128]{2,1,0:T(8,128)S(1)} %sum_copies.5), channel_id=1, replica_groups={{0,2,4,6,8,10,12,14,16,18,20,22,24,26,28,30},{1,3,5,7,9,11,13,15,17,19,..., dimensions={0} | all-to-all | bytes 262144 | tf_op jit(solution)/shard_map/all_to_all | solution.py:371
  69.4 0.0 copy-start
  69.4 0.0 copy-start.1
  69.4 0.0 copy-start.2
  69.4 4.2 %collective-permute-start.3 = (f32[16,16,128]{2,1,0:T(8,128)S(1)}, f32[16,16,128]{2,1,0:T(8,128)S(1)}, u32[]{:S(2)}, u32[]{:S(2)}) collective-permute-start(f32[16,16,128]{2,1,0:T(8,128)S(1)} %all_to_all.29.sums.sums_own), channel_id=1, source_target_pairs={{0,1},{1,0},{2,3},{3,2},{4,5},{5,4},{6,7},{7,6},{8,9},{9,8},{10,11... | collective-permute-start | bytes 393224 | tf_op jit(solution)/shard_map/ppermute | solution.py:375
  73.7 1.9 %solve.1.inverse = f32[64,64]{1,0:T(8,128)S(1)} custom-call(f32[16,16,128]{2,1,0:T(8,128)S(1)} %all_to_all.29.sums.sums_own), custom_call_target="tpu_custom_call" | custom-call | flops 4000000000 | bytes 62500000 | tf_op jit(solution)/shard_map/solve/pallas_call | solution.py:278
  75.6 0.0 collective-permute-done.3.sums_other
  75.6 0.0 copy-done
  75.6 0.0 copy-done.1
  75.6 0.0 copy-done.2
  75.6 4.2 %final.1 = (bf16[1,1024,512]{2,1,0:T(8,128)(2,1)}, f32[64,512]{1,0:T(8,128)}, f32[1024,512]{1,0:T(8,128)}, bf16[1024,512]{1,0:T(8,128)(2,1)}, bf16[1024,512]{1,0:T(8,128)(2,1)}) custom-call(s32[1]{0:T(128)} %bitcast.core, bf16[1024,512]{1,0:T(8,128)(2,1)S(1)} %get-tuple-element.16.g_all.grads, bf16[1024,512]{1,0:T(8,128)(2,1)S(1)} %get-tuple-element.17.e_all.errors, ...), custom_call_target="tpu_custom_call" | custom-call | flops 400000000 | bytes 6250000 | tf_op jit(solution)/shard_map/final/pallas_call | solution.py:342
  (5 shorter events, 0.1 us)
Async XLA Ops:
  2.6 4.3 %collective-permute-start = (f32[4,64,128]{2,1,0:T(8,128)S(1)}, f32[4,64,128]{2,1,0:T(8,128)S(1)}, u32[]{:S(2)}, u32[]{:S(2)}) collective-permute-start(f32[4,64,128]{2,1,0:T(8,128)S(1)} %get-tuple-element.19), channel_id=1, source_target_pairs={{0,1},{1,0},{2,3},{3,2},{4,5},{5,4},{6,7},{7,6},{8,9},{9,8},{10,11... | collective-permute-start | bytes 393224 | tf_op jit(solution)/shard_map/ppermute | solution.py:375
  28.7 3.8 %collective-permute-start.1 = (f32[4,64,128]{2,1,0:T(8,128)S(1)}, f32[4,64,128]{2,1,0:T(8,128)S(1)}, u32[]{:S(2)}, u32[]{:S(2)}) collective-permute-start(f32[4,64,128]{2,1,0:T(8,128)S(1)} %bitcast.5), channel_id=1, source_target_pairs={{0,1},{1,0},{2,3},{3,2},{4,5},{5,4},{6,7},{7,6},{8,9},{9,8},{10,11... | collective-permute-start | bytes 393224 | tf_op jit(solution)/shard_map/ppermute | solution.py:375
  32.8 1.4 %collective-permute-start.2 = (f32[16,8,128]{2,1,0:T(8,128)S(1)}, f32[16,8,128]{2,1,0:T(8,128)S(1)}, u32[]{:S(2)}, u32[]{:S(2)}) collective-permute-start(f32[16,8,128]{2,1,0:T(8,128)S(1)} %right_theirs.1), channel_id=1, source_target_pairs={{0,1},{1,0},{2,3},{3,2},{4,5},{5,4},{6,7},{7,6},{8,9},{9,8},{10,11... | collective-permute-start | bytes 196616 | tf_op jit(solution)/shard_map/ppermute | solution.py:375
  69.4 6.2 %copy-start = (f32[1024,512]{1,0:T(8,128)S(1)}, f32[1024,512]{1,0:T(8,128)}, u32[]{:S(2)}) copy-start(f32[1024,512]{1,0:T(8,128)} %weight.1) | copy-start | bytes 6291460
  69.4 6.2 %copy-start.1 = (bf16[1024,512]{1,0:T(8,128)(2,1)S(1)}, bf16[1024,512]{1,0:T(8,128)(2,1)}, u32[]{:S(2)}) copy-start(bf16[1024,512]{1,0:T(8,128)(2,1)} %first.1) | copy-start | bytes 3145732
  69.4 6.2 %copy-start.2 = (bf16[1024,512]{1,0:T(8,128)(2,1)S(1)}, bf16[1024,512]{1,0:T(8,128)(2,1)}, u32[]{:S(2)}) copy-start(bf16[1024,512]{1,0:T(8,128)(2,1)} %second.1) | copy-start | bytes 3145732
  69.4 6.2 %collective-permute-start.3 = (f32[16,16,128]{2,1,0:T(8,128)S(1)}, f32[16,16,128]{2,1,0:T(8,128)S(1)}, u32[]{:S(2)}, u32[]{:S(2)}) collective-permute-start(f32[16,16,128]{2,1,0:T(8,128)S(1)} %all_to_all.29.sums.sums_own), channel_id=1, source_target_pairs={{0,1},{1,0},{2,3},{3,2},{4,5},{5,4},{6,7},{7,6},{8,9},{9,8},{10,11... | collective-permute-start | bytes 393224 | tf_op jit(solution)/shard_map/ppermute | solution.py:375

commit v3 on v2

v3 whole, which is shorter than its diff:
```python
import functools

import jax
import jax.numpy as jnp
from jax import lax
from jax.experimental import pallas as pl
from jax.experimental.pallas import tpu as pltpu
from jax.sharding import PartitionSpec as P

beta_first = 0.9
beta_second = 0.95
learn_rate = 0.05
weight_decay = 0.1
epsilon = 1e-08
correct_first = 1.0 - 0.9**10
correct_second = 1.0 - 0.95**10

ROWS, COLS, RANK, N_REP, N_FSDP = 1024, 512, 64, 32, 8
HALF, N_CHIP, OWN = ROWS // 2, N_REP // 2, ROWS // N_REP
LANES = 128
f32, bf16 = jnp.float32, jnp.bfloat16
NT = (((1,), (1,)), ((), ()))
NN = (((1,), (0,)), ((), ()))
TN = (((0,), (0,)), ((), ()))


def mm(a, b, dims):
    return lax.dot_general(a, b, dims, preferred_element_type=f32)


def split3(x):
    hi = x.astype(bf16)
    rest = x - hi.astype(f32)
    mid = rest.astype(bf16)
    lo = (rest - mid.astype(f32)).astype(bf16)
    return hi, mid, lo


def stack3(x):
    return jnp.concatenate(split3(x), axis=0)


def fold3(x):
    n = x.shape[0] // 3
    return x[:n] + x[n : 2 * n] + x[2 * n :]


def exact(a, b, dims):
    a1, a2, a3 = split3(a)
    b1, b2, b3 = split3(b)
    small = mm(a1, b3, dims) + mm(a3, b1, dims) + mm(a2, b2, dims)
    return small + (mm(a1, b2, dims) + mm(a2, b1, dims)) + mm(a1, b1, dims)


SMEM = pl.BlockSpec(memory_space=pltpu.SMEM)
VMEM = pl.BlockSpec(memory_space=pltpu.VMEM)
ANY = pl.BlockSpec(memory_space=pl.ANY)


def call(body, name, ins, outs, limit, scratch=(), cost=0):
    return pl.pallas_call(
        body,
        in_specs=ins,
        out_specs=[VMEM if m is None else m for _, _, m in outs],
        out_shape=[
            pltpu.VMEM(s, t) if m is None else jax.ShapeDtypeStruct(s, t) for s, t, m in outs
        ],
        scratch_shapes=scratch,
        compiler_params=pltpu.CompilerParams(vmem_limit_bytes=limit << 20),
        cost_estimate=pl.CostEstimate(flops=cost, bytes_accessed=cost // 64, transcendentals=0),
        name=name,
    )


def tile_columns(block, out):
    for k in range(out.shape[0]):
        out[k] = block[:, k * LANES : (k + 1) * LANES]


def merge_body(flip, core, grads, errors, merged, g_half, e_half, sems):
    half = 1 - core[0] if flip else core[0]
    rows = pl.ds(pl.multiple_of(half * HALF, HALF), HALF)
    copies = [
        pltpu.make_async_copy(grads.at[0, rows], g_half, sems.at[0]),
        pltpu.make_async_copy(errors.at[0, rows], e_half, sems.at[1]),
    ]
    for copy in copies:
        copy.start()
    for copy in copies:
        copy.wait()
    merged[...] = g_half[...].astype(f32) + e_half[...].astype(f32)


def in_hbm(x):
    return pltpu.with_memory_space_constraint(x, pltpu.HBM)


def merge_half(flip, core, grads, errors):
    half = (HALF, COLS)
    return call(
        functools.partial(merge_body, flip), "merge_theirs" if flip else "merge_own",
        [SMEM, ANY, ANY], [(half, f32, None), (half, bf16, None), (half, bf16, None)],
        16, [pltpu.SemaphoreType.DMA((2,))], cost=200_000_000,
    )(core, in_hbm(grads), in_hbm(errors))


def add_body(a, b, out):
    out[...] = a[...] + b[...]


def add(a, b):
    return call(add_body, "add", [VMEM, VMEM], [(a.shape, f32, None)], 8)(a, b)[0]


def sum_copies_body(pieces, out):
    total = pieces[0]
    for k in range(1, pieces.shape[0]):
        total = total + pieces[k]
    for k in range(out.shape[0]):
        out[k] = total


def sum_copies(pieces, copies):
    shape = (copies, *pieces.shape[1:])
    return call(sum_copies_body, "sum_copies", [VMEM], [(shape, f32, None)], 4)(pieces)[0]


def terms_body(pieces, q_prev, factor, out, right):
    merged = pieces[0]
    for k in range(1, N_CHIP):
        merged = merged + pieces[k]
    m_parts = split3(merged)
    left = fold3(mm(jnp.concatenate(m_parts, axis=0), stack3(q_prev[...]), NT))
    left = left[:, :RANK] + left[:, RANK : 2 * RANK] + left[:, 2 * RANK :]
    factor[...] = jnp.concatenate([left[: OWN // 2], left[OWN // 2 :]], axis=1)
    parts = stack3(left.T)
    m1, m2, m3 = m_parts
    right[...] = fold3((mm(parts, m3, NN) + mm(parts, m2, NN)) + mm(parts, m1, NN))
    gram = fold3(mm(parts, parts, NT))
    gram = gram[:, :RANK] + gram[:, RANK : 2 * RANK] + gram[:, 2 * RANK :]
    per = COLS // 2 // LANES
    for r in range(N_REP):
        i, j = divmod(r // 2, per)
        column = LANES * (j + per * (r % 2))
        for k in range(4):
            out[r, k] = right[8 * i + 2 * k : 8 * i + 2 * k + 2, column : column + LANES]
    for p in range(N_CHIP):
        first, second = gram[4 * p : 4 * p + 2], gram[4 * p + 2 : 4 * p + 4]
        both = jnp.concatenate([first, second], axis=1)
        out[2 * p, 4] = both
        out[2 * p + 1, 4] = both


def terms(pieces, q_prev):
    return call(
        terms_body, "terms", [VMEM, VMEM],
        [((OWN // 2, LANES), f32, None), ((N_REP, 5, 2, LANES), f32, None)],
        16, [pltpu.VMEM((RANK, COLS), f32)], cost=100_000_000,
    )(pieces, q_prev.T)


def last_sum_body(pieces, factor, out):
    total = pieces[0]
    for k in range(1, N_FSDP):
        total = total + pieces[k]
    for k in range(N_CHIP):
        for n in range(5):
            out[k, 2 * n : 2 * n + 2] = total[n]
        out[k, 10:16] = jnp.zeros((6, LANES), f32)
        out[k, 16:] = factor[...]


def last_sum(pieces, factor):
    return call(
        last_sum_body, "last_sum", [VMEM, VMEM], [((N_CHIP, 32, LANES), f32, None)], 4
    )(pieces, factor)[0]


def inverse_triangle(gram):
    eye = (
        lax.broadcasted_iota(jnp.int32, (RANK, RANK), 0)
        == lax.broadcasted_iota(jnp.int32, (RANK, RANK), 1)
    ).astype(f32)
    both = jnp.concatenate([gram, eye], axis=1)
    groups = RANK // 8
    rows = [both[8 * g : 8 * g + 8] for g in range(groups)]
    tile = (8, 2 * RANK)
    sub = lax.broadcasted_iota(jnp.int32, tile, 0)
    done = []
    for b in range(groups):
        columns = [
            [
                jnp.broadcast_to(rows[g][:, 8 * b + j : 8 * b + j + 1], tile)
                for g in range(b, groups)
            ]
            for j in range(8)
        ]
        roots = jnp.zeros(tile, f32)
        for k in range(8):
            pivot = jnp.broadcast_to(columns[k][0][k : k + 1], tile)
            inv = 1.0 / pivot
            roots = jnp.where(sub == k, lax.rsqrt(pivot), roots)
            scale = [c * inv for c in columns[k]]
            scale[0] = jnp.where(sub > k, scale[0], 0.0)
            for j in range(k + 1, 8):
                head = jnp.broadcast_to(columns[j][0][k : k + 1], tile)
                columns[j] = [c - x * head for c, x in zip(columns[j], scale)]
            row = jnp.broadcast_to(rows[b][k : k + 1], tile)
            for g in range(b, groups):
                rows[g] = rows[g] - scale[g - b] * row
        done.append(rows[b] * roots)
    return jnp.concatenate(done, axis=0)[:, RANK:]


def solve_body(sums, inverse):
    gram = jnp.concatenate(
        [sums[p, 8:10, half : half + RANK] for p in range(N_CHIP) for half in (0, RANK)], axis=0
    )
    inverse[...] = inverse_triangle(gram)


def solve(sums):
    return call(
        solve_body, "solve", [VMEM], [((RANK, RANK), f32, None)], 4, cost=4_000_000_000
    )(sums)[0]


STEP = 128


def final_body(
    core, g_own, e_own, g_other, e_other, sums_own, sums_other, inverse, weight, first, second,
    new_errors, q_next, new_weight, new_first, new_second,
    right, mix, factor, err_buf, weight_buf, first_buf, second_buf, sems,
):
    half = COLS // 2
    for source, place in ((sums_own, core[0]), (sums_other, 1 - core[0])):
        block = jnp.concatenate(
            [
                jnp.concatenate([source[2 * i, :8], source[2 * i + 1, :8]], axis=1)
                for i in range(RANK // 8)
            ],
            axis=0,
        )
        right[:, pl.ds(pl.multiple_of(place * half, half), half)] = block
        for p in range(N_CHIP):
            n = OWN // 2
            at = pl.multiple_of(place * HALF + OWN * p, OWN)
            factor[pl.ds(at, n)] = source[p, 16:, :RANK]
            factor[pl.ds(at + n, n)] = source[p, 16:, RANK:]
    q_t = exact(inverse[...], right[...], NN) * (1.0 / N_REP)
    q_next[...] = q_t
    w1, w2, w3 = split3(exact(inverse[...], q_t, TN))
    mix[...] = jnp.concatenate([w1, w2, w1, w3, w2, w1], axis=0)

    copies = []
    for step in range(ROWS // STEP):
        other, n = divmod(step * STEP, HALF)
        place = 1 - core[0] if other else core[0]
        grads, errors = (g_other, e_other) if other else (g_own, e_own)
        piece = slice(n, n + STEP)
        rows = pl.ds(pl.multiple_of(place * HALF + n, STEP), STEP)
        f1, f2, f3 = (f.astype(f32) for f in split3(factor[rows]))
        pairs = ((f1, f1), (f2, f1), (f2, f3))
        wide = [jnp.concatenate(pair, axis=1).astype(bf16) for pair in pairs]
        approx = mm(jnp.concatenate(wide, axis=1), mix[...], NN)
        merged = grads[piece].astype(f32) + errors[piece].astype(f32)
        err_buf[rows] = (merged - approx).astype(bf16)
        first_f = beta_first * first[rows].astype(f32) + (1.0 - beta_first) * approx
        second_f = beta_second * second[rows].astype(f32) + ((1.0 - beta_second) * approx) * approx
        first_buf[rows] = first_f.astype(bf16)
        second_buf[rows] = second_f.astype(bf16)
        root = second_f * lax.rsqrt(second_f) * (1.0 / correct_second) ** 0.5 + epsilon
        ratio = (first_f * (learn_rate / correct_first)) / root
        weight_buf[rows] = weight[rows] * (1.0 - learn_rate * weight_decay) - ratio
        for n, (buf, out) in enumerate(
            (
                (err_buf, new_errors.at[0]),
                (weight_buf, new_weight),
                (first_buf, new_first),
                (second_buf, new_second),
            )
        ):
            copy = pltpu.make_async_copy(buf.at[rows], out.at[rows], sems.at[n, step])
            copy.start()
            copies.append(copy)
    for copy in copies:
        copy.wait()


def final(core, own, other, sums_own, sums_other, inverse, weight, first, second):
    wide = (ROWS, COLS)
    return call(
        final_body, "final", [SMEM] + [VMEM] * 10,
        [
            ((1, *wide), bf16, ANY),
            ((RANK, COLS), f32, VMEM),
            (wide, f32, ANY),
            (wide, bf16, ANY),
            (wide, bf16, ANY),
        ],
        16,
        [
            pltpu.VMEM((RANK, COLS), f32),
            pltpu.VMEM((6 * RANK, COLS), bf16),
            pltpu.VMEM((ROWS, RANK), f32),
            pltpu.VMEM(wide, bf16),
            pltpu.VMEM(wide, f32),
            pltpu.VMEM(wide, bf16),
            pltpu.VMEM(wide, bf16),
            pltpu.SemaphoreType.DMA((4, ROWS // STEP)),
        ],
        cost=400_000_000,
    )(core, *own, *other, sums_own, sums_other, inverse, weight, first, second)


PLANE = [[2 * p + c for p in range(N_CHIP)] for c in range(2)]
SWAP = [(i, i ^ 1) for i in range(N_REP)]


def exchange(x):
    return lax.all_to_all(x, "rep", 0, 0, axis_index_groups=PLANE)


def swap(x):
    return lax.ppermute(x, "rep", SWAP)


def shards(grads, errors, q_prev, weight, first_moment, second_moment):
    core = (lax.axis_index("rep") % 2).astype(jnp.int32).reshape(1)
    theirs, *other = merge_half(True, core, grads, errors)
    arrived = swap(theirs)
    mine, *own = merge_half(False, core, grads, errors)
    pieces = exchange(add(mine, arrived).reshape(N_CHIP, OWN, COLS))
    factor, right = terms(pieces, q_prev)
    pieces = sum_copies(lax.all_to_all(right, "rep", 0, 0), N_FSDP)
    pieces = last_sum(lax.all_to_all(pieces, "fsdp", 0, 0), factor)
    sums_own = exchange(pieces)
    sums_other = swap(sums_own)
    inverse = solve(sums_own)
    outs = final(
        core, own, other, sums_own, sums_other, inverse, weight, first_moment, second_moment
    )
    return outs[0], outs[1].T, *outs[2:]


def solution(mesh):
    return jax.shard_map(
        shards,
        mesh=mesh,
        in_specs=(
            P("rep", "fsdp", None),
            P("rep", "fsdp", None),
            P(),
            P("fsdp", None),
            P("fsdp", None),
            P("fsdp", None),
        ),
        out_specs=(P("rep", "fsdp", None), P(), P("fsdp", None), P("fsdp", None), P("fsdp", None)),
        check_vma=False,
    )
```

time: 80.2 us -> 77.7 us (0.969)
  starting transfers between devices: 10.9 us -> 6.66 us
  blocking collectives: 56.9 us -> 59.2 us
    all_to_all x1 -> x2, blocking collectives: 15.2 us -> 28.3 us  [the longest x1 15 us: shards(): pieces = last_sum(lax.all_to_all(pieces, 'fsdp', 0, 0), factor)]
    all_to_all x4 -> x2, blocking collectives: 41.7 us -> 30.9 us  [exchange(): return lax.all_to_all(x, 'rep', 0, 0, axis_index_groups=PLANE)]
    ppermute x4 -> x2, starting transfers between devices: 10.9 us -> 6.66 us  [swap(): return lax.ppermute(x, 'rep', SWAP)]
    pallas_call x7 -> x5, Pallas kernels: 3.64 us -> 3.62 us  [the longest x2 2.68 us: merge_half(): call(functools.partial(merge_body, flip), 'merge_theirs' if flip else 'me...]
  transfers between devices with their start and end apart: 4 -> 2, of which waited for: 3 -> 1; matrix products, arithmetic and copies ran while one was open for 0% -> 0% of each run, Pallas kernels for 4% -> 4%
where the time goes in v3:
time: 77.7 us; the launch traced here: 77.4 us
  blocking collectives  59.2 us (76%)
  Pallas kernels  9.92 us (13%)
  starting transfers between devices  6.66 us (9%)
  waiting for transfers between devices  0.93 us (1%)
    all_to_all x2, blocking collectives, exchange(): return lax.all_to_all(x, 'rep', 0, 0, axis_index_groups=PLANE)  30.9 us
    all_to_all x1, blocking collectives, shards(): pieces = last_sum(lax.all_to_all(pieces, 'fsdp', 0, 0), factor)  15 us
    all_to_all x1, blocking collectives, shards(): pieces = sum_copies(lax.all_to_all(right, 'rep', 0, 0), N_FSDP)  13.4 us
    ppermute x2, starting transfers between devices, swap(): return lax.ppermute(x, 'rep', SWAP)  6.66 us
    pallas_call x1, Pallas kernels, final(): call(final_body, 'final', [SMEM] + [VMEM] * 10, [((1, *wide), bf16, ANY),...  4.34 us
    pallas_call x2, Pallas kernels, merge_half(): call(functools.partial(merge_body, flip), 'merge_theirs' if flip else 'me...  2.68 us
    pallas_call x1, Pallas kernels, solve(): call(solve_body, 'solve', [VMEM], [((RANK, RANK), f32, None)], 4, cost=40...  1.9 us
  transfers between devices with their start and end apart: 2, of which 1 were waited for; matrix products, arithmetic and copies ran while one was open for 0% of the time, Pallas kernels for 4%

profile of v3, /device:TPU:1, one launch (start us, length us, event | category | flops | bytes accessed | tf_op | source)
XLA Modules:
  0.0 77.4 jit_solution(5826197932575700265)
XLA Ops:
  0.6 1.3 %merge_theirs.1 = (f32[512,512]{1,0:T(8,128)S(1)}, bf16[512,512]{1,0:T(8,128)(2,1)S(1)}, bf16[512,512]{1,0:T(8,128)(2,1)S(1)}) custom-call(s32[1]{0:T(128)} %bitcast.core, bf16[1,1024,512]{2,1,0:T(8,128)(2,1)} %grads.3, bf16[1,1024,512]{2,1,0:T(8,128)(2,1)} %errors.3), custom_call_target="tpu_custom_call" | custom-call | flops 200000000 | bytes 3125000 | tf_op jit(solution)/shard_map/merge_theirs/pallas_call | solution.py:100
  2.0 3.3 %collective-permute-start = (f32[512,512]{1,0:T(8,128)S(1)}, f32[512,512]{1,0:T(8,128)S(1)}, u32[]{:S(2)}, u32[]{:S(2)}) collective-permute-start(f32[512,512]{1,0:T(8,128)S(1)} %get-tuple-element.23), channel_id=1, source_target_pairs={{0,1},{1,0},{2,3},{3,2},{4,5},{5,4},{6,7},{7,6},{8,9},{9,8},{10,11... | collective-permute-start | bytes 3145736 | tf_op jit(solution)/shard_map/ppermute | solution.py:326
  5.3 1.4 %merge_own.1 = (f32[512,512]{1,0:T(8,128)S(1)}, bf16[512,512]{1,0:T(8,128)(2,1)S(1)}, bf16[512,512]{1,0:T(8,128)(2,1)S(1)}) custom-call(s32[1]{0:T(128)} %bitcast.core, bf16[1,1024,512]{2,1,0:T(8,128)(2,1)} %grads.3, bf16[1,1024,512]{2,1,0:T(8,128)(2,1)} %errors.3), custom_call_target="tpu_custom_call" | custom-call | flops 200000000 | bytes 3125000 | tf_op jit(solution)/shard_map/merge_own/pallas_call | solution.py:100
  6.7 0.9 %collective-permute-done.b = f32[512,512]{1,0:T(8,128)S(1)} collective-permute-done((f32[512,512]{1,0:T(8,128)S(1)}, f32[512,512]{1,0:T(8,128)S(1)}, u32[]{:S(2)}, u32[]{:S(2)}) %collective-permute-start) | collective-permute-done | bytes 1048608 | tf_op jit(solution)/shard_map/ppermute | solution.py:326
  7.6 0.0 copy-start.3
  7.6 0.1 add.6
  7.7 20.8 %all_to_all.20.pieces = f32[16,32,512]{2,1,0:T(8,128)S(1)} all-to-all(f32[16,32,512]{2,1,0:T(8,128)S(1)} %bitcast.4), channel_id=1, replica_groups={{0,2,4,6,8,10,12,14,16,18,20,22,24,26,28,30},{1,3,5,7,9,11,13,15,17,19,..., dimensions={0} | all-to-all | bytes 2097152 | tf_op jit(solution)/shard_map/all_to_all | solution.py:322
  28.5 0.0 copy-done.3
  28.5 0.8 %terms.1 = (f32[16,128]{1,0:T(8,128)S(1)}, f32[32,5,2,128]{3,2,1,0:T(2,128)S(1)}) custom-call(f32[16,32,512]{2,1,0:T(8,128)S(1)} %all_to_all.20.pieces, f32[64,512]{1,0:T(8,128)S(1)} %bitcast.5), custom_call_target="tpu_custom_call" | custom-call | flops 100000000 | bytes 1562500 | tf_op jit(solution)/shard_map/terms/pallas_call | solution.py:155
  29.3 13.4 %all_to_all.21.pieces = f32[32,5,2,128]{3,2,1,0:T(2,128)S(1)} all-to-all(f32[32,5,2,128]{3,2,1,0:T(2,128)S(1)} %get-tuple-element.24), channel_id=1, replica_groups=mesh['fsdp'=8,'rep'=32] {'rep'}, dimensions={0} | all-to-all | bytes 327680 | tf_op jit(solution)/shard_map/all_to_all | solution.py:336
  42.7 0.1 sum_copies.1
  42.7 15.0 %all_to_all.22.pieces = f32[8,5,2,128]{3,2,1,0:T(2,128)S(1)} all-to-all(f32[8,5,2,128]{3,2,1,0:T(2,128)S(1)} %sum_copies.1), channel_id=1, replica_groups=mesh['fsdp'=8,'rep'=32] {'fsdp'}, dimensions={0} | all-to-all | bytes 81920 | tf_op jit(solution)/shard_map/all_to_all | solution.py:337
  57.7 10.1 %all_to_all.23.sums.sums_own = f32[16,32,128]{2,1,0:T(8,128)S(1)} all-to-all(f32[16,32,128]{2,1,0:T(8,128)S(1)} %last_sum.1), channel_id=1, replica_groups={{0,2,4,6,8,10,12,14,16,18,20,22,24,26,28,30},{1,3,5,7,9,11,13,15,17,19,..., dimensions={0} | all-to-all | bytes 524288 | tf_op jit(solution)/shard_map/all_to_all | solution.py:322
  67.8 0.0 copy-start
  67.8 0.0 copy-start.1
  67.8 0.0 copy-start.2
  67.8 3.3 %collective-permute-start.1 = (f32[16,32,128]{2,1,0:T(8,128)S(1)}, f32[16,32,128]{2,1,0:T(8,128)S(1)}, u32[]{:S(2)}, u32[]{:S(2)}) collective-permute-start(f32[16,32,128]{2,1,0:T(8,128)S(1)} %all_to_all.23.sums.sums_own), channel_id=1, source_target_pairs={{0,1},{1,0},{2,3},{3,2},{4,5},{5,4},{6,7},{7,6},{8,9},{9,8},{10,11... | collective-permute-start | bytes 786440 | tf_op jit(solution)/shard_map/ppermute | solution.py:326
  71.2 1.9 %solve.1.inverse = f32[64,64]{1,0:T(8,128)S(1)} custom-call(f32[16,32,128]{2,1,0:T(8,128)S(1)} %all_to_all.23.sums.sums_own), custom_call_target="tpu_custom_call" | custom-call | flops 4000000000 | bytes 62500000 | tf_op jit(solution)/shard_map/solve/pallas_call | solution.py:223
  73.1 0.0 collective-permute-done.1.sums_other
  73.1 0.0 copy-done
  73.1 0.0 copy-done.1
  73.1 0.0 copy-done.2
  73.1 4.3 %final.1 = (bf16[1,1024,512]{2,1,0:T(8,128)(2,1)}, f32[64,512]{1,0:T(8,128)}, f32[1024,512]{1,0:T(8,128)}, bf16[1024,512]{1,0:T(8,128)(2,1)}, bf16[1024,512]{1,0:T(8,128)(2,1)}) custom-call(s32[1]{0:T(128)} %bitcast.core, bf16[512,512]{1,0:T(8,128)(2,1)S(1)} %get-tuple-element.18.g_own, bf16[512,512]{1,0:T(8,128)(2,1)S(1)} %get-tuple-element.19.e_own, ...), custom_call_target="tpu_custom_call" | custom-call | flops 400000000 | bytes 6250000 | tf_op jit(solution)/shard_map/final/pallas_call | solution.py:293
  (1 shorter events, 0.0 us)
Async XLA Ops:
  2.0 5.6 %collective-permute-start = (f32[512,512]{1,0:T(8,128)S(1)}, f32[512,512]{1,0:T(8,128)S(1)}, u32[]{:S(2)}, u32[]{:S(2)}) collective-permute-start(f32[512,512]{1,0:T(8,128)S(1)} %get-tuple-element.23), channel_id=1, source_target_pairs={{0,1},{1,0},{2,3},{3,2},{4,5},{5,4},{6,7},{7,6},{8,9},{9,8},{10,11... | collective-permute-start | bytes 3145736 | tf_op jit(solution)/shard_map/ppermute | solution.py:326
  7.6 20.9 %copy-start.3 = (f32[512,64]{0,1:T(8,128)S(1)}, f32[512,64]{0,1:T(8,128)}, u32[]{:S(2)}) copy-start(f32[512,64]{0,1:T(8,128)} %param.8) | copy-start | bytes 393220
  67.8 5.2 %copy-start = (f32[1024,512]{1,0:T(8,128)S(1)}, f32[1024,512]{1,0:T(8,128)}, u32[]{:S(2)}) copy-start(f32[1024,512]{1,0:T(8,128)} %weight.1) | copy-start | bytes 6291460
  67.8 5.2 %copy-start.1 = (bf16[1024,512]{1,0:T(8,128)(2,1)S(1)}, bf16[1024,512]{1,0:T(8,128)(2,1)}, u32[]{:S(2)}) copy-start(bf16[1024,512]{1,0:T(8,128)(2,1)} %first.1) | copy-start | bytes 3145732
  67.8 5.3 %copy-start.2 = (bf16[1024,512]{1,0:T(8,128)(2,1)S(1)}, bf16[1024,512]{1,0:T(8,128)(2,1)}, u32[]{:S(2)}) copy-start(bf16[1024,512]{1,0:T(8,128)(2,1)} %second.1) | copy-start | bytes 3145732
  67.8 5.2 %collective-permute-start.1 = (f32[16,32,128]{2,1,0:T(8,128)S(1)}, f32[16,32,128]{2,1,0:T(8,128)S(1)}, u32[]{:S(2)}, u32[]{:S(2)}) collective-permute-start(f32[16,32,128]{2,1,0:T(8,128)S(1)} %all_to_all.23.sums.sums_own), channel_id=1, source_target_pairs={{0,1},{1,0},{2,3},{3,2},{4,5},{5,4},{6,7},{7,6},{8,9},{9,8},{10,11... | collective-permute-start | bytes 786440 | tf_op jit(solution)/shard_map/ppermute | solution.py:326

commit v4 on v3

--- a/solution.py
+++ b/solution.py
@@ -77,31 +77,42 @@
         out[k] = block[:, k * LANES : (k + 1) * LANES]
 
 
-def merge_body(flip, core, grads, errors, merged, g_half, e_half, sems):
+def merge_body(flip, core, grads, errors, *refs):
+    if flip:
+        merged, g_half, e_half, sems = refs
+        copies = []
+    else:
+        weight, merged, g_half, e_half, weight_kept, sems = refs
+        copies = [pltpu.make_async_copy(weight, weight_kept, sems.at[2])]
     half = 1 - core[0] if flip else core[0]
     rows = pl.ds(pl.multiple_of(half * HALF, HALF), HALF)
-    copies = [
+    pair = [
         pltpu.make_async_copy(grads.at[0, rows], g_half, sems.at[0]),
         pltpu.make_async_copy(errors.at[0, rows], e_half, sems.at[1]),
     ]
-    for copy in copies:
+    for copy in pair + copies:
         copy.start()
+    for copy in pair:
+        copy.wait()
+    merged[...] = g_half[...].astype(f32) + e_half[...].astype(f32)
     for copy in copies:
         copy.wait()
-    merged[...] = g_half[...].astype(f32) + e_half[...].astype(f32)
 
 
 def in_hbm(x):
     return pltpu.with_memory_space_constraint(x, pltpu.HBM)
 
 
-def merge_half(flip, core, grads, errors):
+def merge_half(flip, core, *arrays):
     half = (HALF, COLS)
+    outs = [(half, f32, None), (half, bf16, None), (half, bf16, None)]
+    if not flip:
+        outs.append(((ROWS, COLS), f32, None))
     return call(
         functools.partial(merge_body, flip), "merge_theirs" if flip else "merge_own",
-        [SMEM, ANY, ANY], [(half, f32, None), (half, bf16, None), (half, bf16, None)],
-        16, [pltpu.SemaphoreType.DMA((2,))], cost=200_000_000,
-    )(core, in_hbm(grads), in_hbm(errors))
+        [SMEM] + [ANY] * len(arrays), outs,
+        16, [pltpu.SemaphoreType.DMA((3,))], cost=200_000_000,
+    )(core, *(in_hbm(x) for x in arrays))
 
 
 def add_body(a, b, out):
@@ -176,6 +187,9 @@
     )(pieces, factor)[0]
 
 
+PANEL = 16
+
+
 def inverse_triangle(gram):
     eye = (
         lax.broadcasted_iota(jnp.int32, (RANK, RANK), 0)
@@ -186,29 +200,30 @@
     rows = [both[8 * g : 8 * g + 8] for g in range(groups)]
     tile = (8, 2 * RANK)
     sub = lax.broadcasted_iota(jnp.int32, tile, 0)
-    done = []
-    for b in range(groups):
+    pivots = [jnp.ones(tile, f32)] * groups
+    for start in range(0, RANK, PANEL):
         columns = [
-            [
-                jnp.broadcast_to(rows[g][:, 8 * b + j : 8 * b + j + 1], tile)
-                for g in range(b, groups)
-            ]
-            for j in range(8)
+            {
+                g: jnp.broadcast_to(rows[g][:, start + j : start + j + 1], tile)
+                for g in range(start // 8, groups)
+            }
+            for j in range(PANEL)
         ]
-        roots = jnp.zeros(tile, f32)
-        for k in range(8):
-            pivot = jnp.broadcast_to(columns[k][0][k : k + 1], tile)
+        for k in range(PANEL):
+            at, line = divmod(start + k, 8)
+            pivot = jnp.broadcast_to(columns[k][at][line : line + 1], tile)
             inv = 1.0 / pivot
-            roots = jnp.where(sub == k, lax.rsqrt(pivot), roots)
-            scale = [c * inv for c in columns[k]]
-            scale[0] = jnp.where(sub > k, scale[0], 0.0)
-            for j in range(k + 1, 8):
-                head = jnp.broadcast_to(columns[j][0][k : k + 1], tile)
-                columns[j] = [c - x * head for c, x in zip(columns[j], scale)]
-            row = jnp.broadcast_to(rows[b][k : k + 1], tile)
-            for g in range(b, groups):
-                rows[g] = rows[g] - scale[g - b] * row
-        done.append(rows[b] * roots)
+            pivots[at] = jnp.where(sub == line, pivot, pivots[at])
+            scale = {g: c * inv for g, c in columns[k].items() if g >= at}
+            scale[at] = jnp.where(sub > line, scale[at], 0.0)
+            for j in range(k + 1, PANEL):
+                head = jnp.broadcast_to(columns[j][at][line : line + 1], tile)
+                for g in scale:
+                    columns[j][g] = columns[j][g] - scale[g] * head
+            row = jnp.broadcast_to(rows[at][line : line + 1], tile)
+            for g in scale:
+                rows[g] = rows[g] - scale[g] * row
+    done = [row * lax.rsqrt(pivot) for row, pivot in zip(rows, pivots)]
     return jnp.concatenate(done, axis=0)[:, RANK:]
 
 
@@ -330,7 +345,7 @@
     core = (lax.axis_index("rep") % 2).astype(jnp.int32).reshape(1)
     theirs, *other = merge_half(True, core, grads, errors)
     arrived = swap(theirs)
-    mine, *own = merge_half(False, core, grads, errors)
+    mine, *own, weight = merge_half(False, core, grads, errors, weight)
     pieces = exchange(add(mine, arrived).reshape(N_CHIP, OWN, COLS))
     factor, right = terms(pieces, q_prev)
     pieces = sum_copies(lax.all_to_all(right, "rep", 0, 0), N_FSDP)

time: 77.7 us -> 77.5 us (level)
  transfers between devices with their start and end apart: 2 -> 2, of which waited for: 1 -> 1; matrix products, arithmetic and copies ran while one was open for 0% -> 0% of each run, Pallas kernels for 4% -> 5%
where the time goes in v4:
time: 77.5 us; the launch traced here: 77.3 us
  blocking collectives  59.2 us (76%)
  Pallas kernels  10.4 us (13%)
  starting transfers between devices  6.66 us (9%)
    all_to_all x2, blocking collectives, exchange(): return lax.all_to_all(x, 'rep', 0, 0, axis_index_groups=PLANE)  30.9 us
    all_to_all x1, blocking collectives, shards(): pieces = last_sum(lax.all_to_all(pieces, 'fsdp', 0, 0), factor)  15 us
    all_to_all x1, blocking collectives, shards(): pieces = sum_copies(lax.all_to_all(right, 'rep', 0, 0), N_FSDP)  13.4 us
    ppermute x2, starting transfers between devices, swap(): return lax.ppermute(x, 'rep', SWAP)  6.66 us
    pallas_call x1, Pallas kernels, final(): call(final_body, 'final', [SMEM] + [VMEM] * 10, [((1, *wide), bf16, ANY),...  4.33 us
    pallas_call x2, Pallas kernels, merge_half(): call(functools.partial(merge_body, flip), 'merge_theirs' if flip else 'me...  3.28 us
    pallas_call x1, Pallas kernels, solve(): call(solve_body, 'solve', [VMEM], [((RANK, RANK), f32, None)], 4, cost=40...  1.74 us
  transfers between devices with their start and end apart: 2, of which 1 were waited for; matrix products, arithmetic and copies ran while one was open for 0% of the time, Pallas kernels for 5%

profile of v4, /device:TPU:1, one launch (start us, length us, event | category | flops | bytes accessed | tf_op | source)
XLA Modules:
  0.0 77.3 jit_solution(6903360622554163341)
XLA Ops:
  0.6 1.3 %merge_theirs.1 = (f32[512,512]{1,0:T(8,128)S(1)}, bf16[512,512]{1,0:T(8,128)(2,1)S(1)}, bf16[512,512]{1,0:T(8,128)(2,1)S(1)}) custom-call(s32[1]{0:T(128)} %bitcast.core, bf16[1,1024,512]{2,1,0:T(8,128)(2,1)} %grads.3, bf16[1,1024,512]{2,1,0:T(8,128)(2,1)} %errors.3), custom_call_target="tpu_custom_call" | custom-call | flops 200000000 | bytes 3125000 | tf_op jit(solution)/shard_map/merge_theirs/pallas_call | solution.py:111
  2.0 3.3 %collective-permute-start = (f32[512,512]{1,0:T(8,128)S(1)}, f32[512,512]{1,0:T(8,128)S(1)}, u32[]{:S(2)}, u32[]{:S(2)}) collective-permute-start(f32[512,512]{1,0:T(8,128)S(1)} %get-tuple-element.24), channel_id=1, source_target_pairs={{0,1},{1,0},{2,3},{3,2},{4,5},{5,4},{6,7},{7,6},{8,9},{9,8},{10,11... | collective-permute-start | bytes 3145736 | tf_op jit(solution)/shard_map/ppermute | solution.py:341
  5.3 1.9 %merge_own.1 = (f32[512,512]{1,0:T(8,128)S(1)}, bf16[512,512]{1,0:T(8,128)(2,1)S(1)}, bf16[512,512]{1,0:T(8,128)(2,1)S(1)}, f32[1024,512]{1,0:T(8,128)S(1)}) custom-call(s32[1]{0:T(128)} %bitcast.core, bf16[1,1024,512]{2,1,0:T(8,128)(2,1)} %grads.3, bf16[1,1024,512]{2,1,0:T(8,128)(2,1)} %errors.3, f32[1024,512]{1,0:T(8,128)} %refs_0_.1), custom_call_target="tpu_custom_call" | custom-call | flops 200000000 | bytes 3125000 | tf_op jit(solution)/shard_map/merge_own/pallas_call | solution.py:111
  7.3 0.3 collective-permute-done.b
  7.6 0.0 copy-start.2
  7.6 0.1 add.6
  7.7 20.8 %all_to_all.20.pieces = f32[16,32,512]{2,1,0:T(8,128)S(1)} all-to-all(f32[16,32,512]{2,1,0:T(8,128)S(1)} %bitcast.4), channel_id=1, replica_groups={{0,2,4,6,8,10,12,14,16,18,20,22,24,26,28,30},{1,3,5,7,9,11,13,15,17,19,..., dimensions={0} | all-to-all | bytes 2097152 | tf_op jit(solution)/shard_map/all_to_all | solution.py:337
  28.5 0.0 copy-done.2
  28.5 0.8 %terms.1 = (f32[16,128]{1,0:T(8,128)S(1)}, f32[32,5,2,128]{3,2,1,0:T(2,128)S(1)}) custom-call(f32[16,32,512]{2,1,0:T(8,128)S(1)} %all_to_all.20.pieces, f32[64,512]{1,0:T(8,128)S(1)} %bitcast.5), custom_call_target="tpu_custom_call" | custom-call | flops 100000000 | bytes 1562500 | tf_op jit(solution)/shard_map/terms/pallas_call | solution.py:166
  29.3 13.4 %all_to_all.21.pieces = f32[32,5,2,128]{3,2,1,0:T(2,128)S(1)} all-to-all(f32[32,5,2,128]{3,2,1,0:T(2,128)S(1)} %get-tuple-element.25), channel_id=1, replica_groups=mesh['fsdp'=8,'rep'=32] {'rep'}, dimensions={0} | all-to-all | bytes 327680 | tf_op jit(solution)/shard_map/all_to_all | solution.py:351
  42.7 0.1 sum_copies.1
  42.7 15.0 %all_to_all.22.pieces = f32[8,5,2,128]{3,2,1,0:T(2,128)S(1)} all-to-all(f32[8,5,2,128]{3,2,1,0:T(2,128)S(1)} %sum_copies.1), channel_id=1, replica_groups=mesh['fsdp'=8,'rep'=32] {'fsdp'}, dimensions={0} | all-to-all | bytes 81920 | tf_op jit(solution)/shard_map/all_to_all | solution.py:352
  57.8 10.1 %all_to_all.23.sums.sums_own = f32[16,32,128]{2,1,0:T(8,128)S(1)} all-to-all(f32[16,32,128]{2,1,0:T(8,128)S(1)} %last_sum.1), channel_id=1, replica_groups={{0,2,4,6,8,10,12,14,16,18,20,22,24,26,28,30},{1,3,5,7,9,11,13,15,17,19,..., dimensions={0} | all-to-all | bytes 524288 | tf_op jit(solution)/shard_map/all_to_all | solution.py:337
  67.8 0.0 copy-start
  67.8 0.0 copy-start.1
  67.8 3.3 %collective-permute-start.1 = (f32[16,32,128]{2,1,0:T(8,128)S(1)}, f32[16,32,128]{2,1,0:T(8,128)S(1)}, u32[]{:S(2)}, u32[]{:S(2)}) collective-permute-start(f32[16,32,128]{2,1,0:T(8,128)S(1)} %all_to_all.23.sums.sums_own), channel_id=1, source_target_pairs={{0,1},{1,0},{2,3},{3,2},{4,5},{5,4},{6,7},{7,6},{8,9},{9,8},{10,11... | collective-permute-start | bytes 786440 | tf_op jit(solution)/shard_map/ppermute | solution.py:341
  71.2 1.7 %solve.1.inverse = f32[64,64]{1,0:T(8,128)S(1)} custom-call(f32[16,32,128]{2,1,0:T(8,128)S(1)} %all_to_all.23.sums.sums_own), custom_call_target="tpu_custom_call" | custom-call | flops 4000000000 | bytes 62500000 | tf_op jit(solution)/shard_map/solve/pallas_call | solution.py:238
  72.9 0.0 collective-permute-done.1.sums_other
  72.9 0.0 copy-done
  72.9 0.0 copy-done.1
  72.9 4.3 %final.1 = (bf16[1,1024,512]{2,1,0:T(8,128)(2,1)}, f32[64,512]{1,0:T(8,128)}, f32[1024,512]{1,0:T(8,128)}, bf16[1024,512]{1,0:T(8,128)(2,1)}, bf16[1024,512]{1,0:T(8,128)(2,1)}) custom-call(s32[1]{0:T(128)} %bitcast.core, bf16[512,512]{1,0:T(8,128)(2,1)S(1)} %get-tuple-element.19.g_own, bf16[512,512]{1,0:T(8,128)(2,1)S(1)} %get-tuple-element.20.e_own, ...), custom_call_target="tpu_custom_call" | custom-call | flops 400000000 | bytes 6250000 | tf_op jit(solution)/shard_map/final/pallas_call | solution.py:308
  (1 shorter events, 0.0 us)
Async XLA Ops:
  2.0 5.6 %collective-permute-start = (f32[512,512]{1,0:T(8,128)S(1)}, f32[512,512]{1,0:T(8,128)S(1)}, u32[]{:S(2)}, u32[]{:S(2)}) collective-permute-start(f32[512,512]{1,0:T(8,128)S(1)} %get-tuple-element.24), channel_id=1, source_target_pairs={{0,1},{1,0},{2,3},{3,2},{4,5},{5,4},{6,7},{7,6},{8,9},{9,8},{10,11... | collective-permute-start | bytes 3145736 | tf_op jit(solution)/shard_map/ppermute | solution.py:341
  7.6 20.9 %copy-start.2 = (f32[512,64]{0,1:T(8,128)S(1)}, f32[512,64]{0,1:T(8,128)}, u32[]{:S(2)}) copy-start(f32[512,64]{0,1:T(8,128)} %param.8) | copy-start | bytes 393220
  67.8 5.1 %copy-start = (bf16[1024,512]{1,0:T(8,128)(2,1)S(1)}, bf16[1024,512]{1,0:T(8,128)(2,1)}, u32[]{:S(2)}) copy-start(bf16[1024,512]{1,0:T(8,128)(2,1)} %first.1) | copy-start | bytes 3145732
  67.8 5.1 %copy-start.1 = (bf16[1024,512]{1,0:T(8,128)(2,1)S(1)}, bf16[1024,512]{1,0:T(8,128)(2,1)}, u32[]{:S(2)}) copy-start(bf16[1024,512]{1,0:T(8,128)(2,1)} %second.1) | copy-start | bytes 3145732
  67.8 5.1 %collective-permute-start.1 = (f32[16,32,128]{2,1,0:T(8,128)S(1)}, f32[16,32,128]{2,1,0:T(8,128)S(1)}, u32[]{:S(2)}, u32[]{:S(2)}) collective-permute-start(f32[16,32,128]{2,1,0:T(8,128)S(1)} %all_to_all.23.sums.sums_own), channel_id=1, source_target_pairs={{0,1},{1,0},{2,3},{3,2},{4,5},{5,4},{6,7},{7,6},{8,9},{9,8},{10,11... | collective-permute-start | bytes 786440 | tf_op jit(solution)/shard_map/ppermute | solution.py:341

commit v5 on v4

--- a/solution.py
+++ b/solution.py
@@ -45,11 +45,15 @@
     return x[:n] + x[n : 2 * n] + x[2 * n :]
 
 
-def exact(a, b, dims):
-    a1, a2, a3 = split3(a)
-    b1, b2, b3 = split3(b)
-    small = mm(a1, b3, dims) + mm(a3, b1, dims) + mm(a2, b2, dims)
-    return small + (mm(a1, b2, dims) + mm(a2, b1, dims)) + mm(a1, b1, dims)
+def left_pieces(x):
+    x1, x2, x3 = (p.astype(f32) for p in split3(x))
+    pairs = ((x1, x1), (x2, x1), (x2, x3))
+    return jnp.concatenate([jnp.concatenate(p, axis=1).astype(bf16) for p in pairs], axis=1)
+
+
+def right_pieces(x):
+    x1, x2, x3 = split3(x)
+    return jnp.concatenate([x1, x2, x1, x3, x2, x1], axis=0)
 
 
 SMEM = pl.BlockSpec(memory_space=pltpu.SMEM)
@@ -70,11 +74,6 @@
         cost_estimate=pl.CostEstimate(flops=cost, bytes_accessed=cost // 64, transcendentals=0),
         name=name,
     )
-
-
-def tile_columns(block, out):
-    for k in range(out.shape[0]):
-        out[k] = block[:, k * LANES : (k + 1) * LANES]
 
 
 def merge_body(flip, core, grads, errors, *refs):
@@ -263,10 +262,9 @@
             at = pl.multiple_of(place * HALF + OWN * p, OWN)
             factor[pl.ds(at, n)] = source[p, 16:, :RANK]
             factor[pl.ds(at + n, n)] = source[p, 16:, RANK:]
-    q_t = exact(inverse[...], right[...], NN) * (1.0 / N_REP)
+    q_t = mm(left_pieces(inverse[...]), right_pieces(right[...]), NN) * (1.0 / N_REP)
     q_next[...] = q_t
-    w1, w2, w3 = split3(exact(inverse[...], q_t, TN))
-    mix[...] = jnp.concatenate([w1, w2, w1, w3, w2, w1], axis=0)
+    mix[...] = right_pieces(mm(left_pieces(inverse[...].T), right_pieces(q_t), NN))
 
     copies = []
     for step in range(ROWS // STEP):
@@ -275,10 +273,7 @@
         grads, errors = (g_other, e_other) if other else (g_own, e_own)
         piece = slice(n, n + STEP)
         rows = pl.ds(pl.multiple_of(place * HALF + n, STEP), STEP)
-        f1, f2, f3 = (f.astype(f32) for f in split3(factor[rows]))
-        pairs = ((f1, f1), (f2, f1), (f2, f3))
-        wide = [jnp.concatenate(pair, axis=1).astype(bf16) for pair in pairs]
-        approx = mm(jnp.concatenate(wide, axis=1), mix[...], NN)
+        approx = mm(left_pieces(factor[rows]), mix[...], NN)
         merged = grads[piece].astype(f32) + errors[piece].astype(f32)
         err_buf[rows] = (merged - approx).astype(bf16)
         first_f = beta_first * first[rows].astype(f32) + (1.0 - beta_first) * approx

time: 77.5 us -> 77.5 us (level)
  no operation moved by 1% of the time
where the time goes in v5:
time: 77.5 us; the launch traced here: 77.2 us
  blocking collectives  59.2 us (76%)
  Pallas kernels  10.3 us (13%)
  starting transfers between devices  6.66 us (9%)
    all_to_all x2, blocking collectives, exchange(): return lax.all_to_all(x, 'rep', 0, 0, axis_index_groups=PLANE)  30.9 us
    all_to_all x1, blocking collectives, shards(): pieces = last_sum(lax.all_to_all(pieces, 'fsdp', 0, 0), factor)  15 us
    all_to_all x1, blocking collectives, shards(): pieces = sum_copies(lax.all_to_all(right, 'rep', 0, 0), N_FSDP)  13.4 us
    ppermute x2, starting transfers between devices, swap(): return lax.ppermute(x, 'rep', SWAP)  6.66 us
    pallas_call x1, Pallas kernels, final(): call(final_body, 'final', [SMEM] + [VMEM] * 10, [((1, *wide), bf16, ANY),...  4.26 us
    pallas_call x2, Pallas kernels, merge_half(): call(functools.partial(merge_body, flip), 'merge_theirs' if flip else 'me...  3.28 us
    pallas_call x1, Pallas kernels, solve(): call(solve_body, 'solve', [VMEM], [((RANK, RANK), f32, None)], 4, cost=40...  1.74 us
  transfers between devices with their start and end apart: 2, of which 1 were waited for; matrix products, arithmetic and copies ran while one was open for 0% of the time, Pallas kernels for 5%

profile of v5, /device:TPU:1, one launch (start us, length us, event | category | flops | bytes accessed | tf_op | source)
XLA Modules:
  0.0 77.2 jit_solution(7752876315109045681)
XLA Ops:
  0.6 1.3 %merge_theirs.1 = (f32[512,512]{1,0:T(8,128)S(1)}, bf16[512,512]{1,0:T(8,128)(2,1)S(1)}, bf16[512,512]{1,0:T(8,128)(2,1)S(1)}) custom-call(s32[1]{0:T(128)} %bitcast.core, bf16[1,1024,512]{2,1,0:T(8,128)(2,1)} %grads.3, bf16[1,1024,512]{2,1,0:T(8,128)(2,1)} %errors.3), custom_call_target="tpu_custom_call" | custom-call | flops 200000000 | bytes 3125000 | tf_op jit(solution)/shard_map/merge_theirs/pallas_call | solution.py:110
  2.0 3.3 %collective-permute-start = (f32[512,512]{1,0:T(8,128)S(1)}, f32[512,512]{1,0:T(8,128)S(1)}, u32[]{:S(2)}, u32[]{:S(2)}) collective-permute-start(f32[512,512]{1,0:T(8,128)S(1)} %get-tuple-element.24), channel_id=1, source_target_pairs={{0,1},{1,0},{2,3},{3,2},{4,5},{5,4},{6,7},{7,6},{8,9},{9,8},{10,11... | collective-permute-start | bytes 3145736 | tf_op jit(solution)/shard_map/ppermute | solution.py:336
  5.3 1.9 %merge_own.1 = (f32[512,512]{1,0:T(8,128)S(1)}, bf16[512,512]{1,0:T(8,128)(2,1)S(1)}, bf16[512,512]{1,0:T(8,128)(2,1)S(1)}, f32[1024,512]{1,0:T(8,128)S(1)}) custom-call(s32[1]{0:T(128)} %bitcast.core, bf16[1,1024,512]{2,1,0:T(8,128)(2,1)} %grads.3, bf16[1,1024,512]{2,1,0:T(8,128)(2,1)} %errors.3, f32[1024,512]{1,0:T(8,128)} %refs_0_.1), custom_call_target="tpu_custom_call" | custom-call | flops 200000000 | bytes 3125000 | tf_op jit(solution)/shard_map/merge_own/pallas_call | solution.py:110
  7.3 0.3 collective-permute-done.b
  7.6 0.0 copy-start.2
  7.6 0.1 add.6
  7.7 20.8 %all_to_all.20.pieces = f32[16,32,512]{2,1,0:T(8,128)S(1)} all-to-all(f32[16,32,512]{2,1,0:T(8,128)S(1)} %bitcast.4), channel_id=1, replica_groups={{0,2,4,6,8,10,12,14,16,18,20,22,24,26,28,30},{1,3,5,7,9,11,13,15,17,19,..., dimensions={0} | all-to-all | bytes 2097152 | tf_op jit(solution)/shard_map/all_to_all | solution.py:332
  28.5 0.0 copy-done.2
  28.5 0.8 %terms.1 = (f32[16,128]{1,0:T(8,128)S(1)}, f32[32,5,2,128]{3,2,1,0:T(2,128)S(1)}) custom-call(f32[16,32,512]{2,1,0:T(8,128)S(1)} %all_to_all.20.pieces, f32[64,512]{1,0:T(8,128)S(1)} %bitcast.5), custom_call_target="tpu_custom_call" | custom-call | flops 100000000 | bytes 1562500 | tf_op jit(solution)/shard_map/terms/pallas_call | solution.py:165
  29.3 13.4 %all_to_all.21.pieces = f32[32,5,2,128]{3,2,1,0:T(2,128)S(1)} all-to-all(f32[32,5,2,128]{3,2,1,0:T(2,128)S(1)} %get-tuple-element.25), channel_id=1, replica_groups=mesh['fsdp'=8,'rep'=32] {'rep'}, dimensions={0} | all-to-all | bytes 327680 | tf_op jit(solution)/shard_map/all_to_all | solution.py:346
  42.7 0.1 sum_copies.1
  42.7 15.0 %all_to_all.22.pieces = f32[8,5,2,128]{3,2,1,0:T(2,128)S(1)} all-to-all(f32[8,5,2,128]{3,2,1,0:T(2,128)S(1)} %sum_copies.1), channel_id=1, replica_groups=mesh['fsdp'=8,'rep'=32] {'fsdp'}, dimensions={0} | all-to-all | bytes 81920 | tf_op jit(solution)/shard_map/all_to_all | solution.py:347
  57.8 10.1 %all_to_all.23.sums.sums_own = f32[16,32,128]{2,1,0:T(8,128)S(1)} all-to-all(f32[16,32,128]{2,1,0:T(8,128)S(1)} %last_sum.1), channel_id=1, replica_groups={{0,2,4,6,8,10,12,14,16,18,20,22,24,26,28,30},{1,3,5,7,9,11,13,15,17,19,..., dimensions={0} | all-to-all | bytes 524288 | tf_op jit(solution)/shard_map/all_to_all | solution.py:332
  67.8 0.0 copy-start
  67.8 0.0 copy-start.1
  67.8 3.3 %collective-permute-start.1 = (f32[16,32,128]{2,1,0:T(8,128)S(1)}, f32[16,32,128]{2,1,0:T(8,128)S(1)}, u32[]{:S(2)}, u32[]{:S(2)}) collective-permute-start(f32[16,32,128]{2,1,0:T(8,128)S(1)} %all_to_all.23.sums.sums_own), channel_id=1, source_target_pairs={{0,1},{1,0},{2,3},{3,2},{4,5},{5,4},{6,7},{7,6},{8,9},{9,8},{10,11... | collective-permute-start | bytes 786440 | tf_op jit(solution)/shard_map/ppermute | solution.py:336
  71.2 1.7 %solve.1.inverse = f32[64,64]{1,0:T(8,128)S(1)} custom-call(f32[16,32,128]{2,1,0:T(8,128)S(1)} %all_to_all.23.sums.sums_own), custom_call_target="tpu_custom_call" | custom-call | flops 4000000000 | bytes 62500000 | tf_op jit(solution)/shard_map/solve/pallas_call | solution.py:237
  72.9 0.0 collective-permute-done.1.sums_other
  72.9 0.0 copy-done
  72.9 0.0 copy-done.1
  72.9 4.3 %final.1 = (bf16[1,1024,512]{2,1,0:T(8,128)(2,1)}, f32[64,512]{1,0:T(8,128)}, f32[1024,512]{1,0:T(8,128)}, bf16[1024,512]{1,0:T(8,128)(2,1)}, bf16[1024,512]{1,0:T(8,128)(2,1)}) custom-call(s32[1]{0:T(128)} %bitcast.core, bf16[512,512]{1,0:T(8,128)(2,1)S(1)} %get-tuple-element.19.g_own, bf16[512,512]{1,0:T(8,128)(2,1)S(1)} %get-tuple-element.20.e_own, ...), custom_call_target="tpu_custom_call" | custom-call | flops 400000000 | bytes 6250000 | tf_op jit(solution)/shard_map/final/pallas_call | solution.py:303
  (1 shorter events, 0.0 us)
Async XLA Ops:
  2.0 5.6 %collective-permute-start = (f32[512,512]{1,0:T(8,128)S(1)}, f32[512,512]{1,0:T(8,128)S(1)}, u32[]{:S(2)}, u32[]{:S(2)}) collective-permute-start(f32[512,512]{1,0:T(8,128)S(1)} %get-tuple-element.24), channel_id=1, source_target_pairs={{0,1},{1,0},{2,3},{3,2},{4,5},{5,4},{6,7},{7,6},{8,9},{9,8},{10,11... | collective-permute-start | bytes 3145736 | tf_op jit(solution)/shard_map/ppermute | solution.py:336
  7.6 20.9 %copy-start.2 = (f32[512,64]{0,1:T(8,128)S(1)}, f32[512,64]{0,1:T(8,128)}, u32[]{:S(2)}) copy-start(f32[512,64]{0,1:T(8,128)} %param.8) | copy-start | bytes 393220
  67.8 5.1 %copy-start = (bf16[1024,512]{1,0:T(8,128)(2,1)S(1)}, bf16[1024,512]{1,0:T(8,128)(2,1)}, u32[]{:S(2)}) copy-start(bf16[1024,512]{1,0:T(8,128)(2,1)} %first.1) | copy-start | bytes 3145732
  67.8 5.1 %copy-start.1 = (bf16[1024,512]{1,0:T(8,128)(2,1)S(1)}, bf16[1024,512]{1,0:T(8,128)(2,1)}, u32[]{:S(2)}) copy-start(bf16[1024,512]{1,0:T(8,128)(2,1)} %second.1) | copy-start | bytes 3145732
  67.8 5.1 %collective-permute-start.1 = (f32[16,32,128]{2,1,0:T(8,128)S(1)}, f32[16,32,128]{2,1,0:T(8,128)S(1)}, u32[]{:S(2)}, u32[]{:S(2)}) collective-permute-start(f32[16,32,128]{2,1,0:T(8,128)S(1)} %all_to_all.23.sums.sums_own), channel_id=1, source_target_pairs={{0,1},{1,0},{2,3},{3,2},{4,5},{5,4},{6,7},{7,6},{8,9},{9,8},{10,11... | collective-permute-start | bytes 786440 | tf_op jit(solution)/shard_map/ppermute | solution.py:336

commit v6 on v5

--- a/solution.py
+++ b/solution.py
@@ -175,14 +175,14 @@
         total = total + pieces[k]
     for k in range(N_CHIP):
         for n in range(5):
-            out[k, 2 * n : 2 * n + 2] = total[n]
-        out[k, 10:16] = jnp.zeros((6, LANES), f32)
-        out[k, 16:] = factor[...]
+            out[k, n] = total[n]
+        for n in range(8):
+            out[k, 5 + n] = factor[2 * n : 2 * n + 2]
 
 
 def last_sum(pieces, factor):
     return call(
-        last_sum_body, "last_sum", [VMEM, VMEM], [((N_CHIP, 32, LANES), f32, None)], 4
+        last_sum_body, "last_sum", [VMEM, VMEM], [((N_CHIP, 13, 2, LANES), f32, None)], 4
     )(pieces, factor)[0]
 
 
@@ -226,9 +226,13 @@
     return jnp.concatenate(done, axis=0)[:, RANK:]
 
 
+def stacked(sums, p, start, stop):
+    return jnp.concatenate([sums[p, n] for n in range(start, stop)], axis=0)
+
+
 def solve_body(sums, inverse):
     gram = jnp.concatenate(
-        [sums[p, 8:10, half : half + RANK] for p in range(N_CHIP) for half in (0, RANK)], axis=0
+        [sums[p, 4, :, half : half + RANK] for p in range(N_CHIP) for half in (0, RANK)], axis=0
     )
     inverse[...] = inverse_triangle(gram)
 
@@ -251,7 +255,7 @@
     for source, place in ((sums_own, core[0]), (sums_other, 1 - core[0])):
         block = jnp.concatenate(
             [
-                jnp.concatenate([source[2 * i, :8], source[2 * i + 1, :8]], axis=1)
+                jnp.concatenate([stacked(source, 2 * i, 0, 4), stacked(source, 2 * i + 1, 0, 4)], axis=1)
                 for i in range(RANK // 8)
             ],
             axis=0,
@@ -260,8 +264,9 @@
         for p in range(N_CHIP):
             n = OWN // 2
             at = pl.multiple_of(place * HALF + OWN * p, OWN)
-            factor[pl.ds(at, n)] = source[p, 16:, :RANK]
-            factor[pl.ds(at + n, n)] = source[p, 16:, RANK:]
+            both = stacked(source, p, 5, 13)
+            factor[pl.ds(at, n)] = both[:, :RANK]
+            factor[pl.ds(at + n, n)] = both[:, RANK:]
     q_t = mm(left_pieces(inverse[...]), right_pieces(right[...]), NN) * (1.0 / N_REP)
     q_next[...] = q_t
     mix[...] = right_pieces(mm(left_pieces(inverse[...].T), right_pieces(q_t), NN))

time: 77.5 us -> 77.2 us (level)
  no operation moved by 1% of the time
where the time goes in v6:
time: 77.2 us; the launch traced here: 76.9 us
  blocking collectives  59 us (76%)
  Pallas kernels  10.3 us (13%)
  starting transfers between devices  6.59 us (9%)
    all_to_all x2, blocking collectives, exchange(): return lax.all_to_all(x, 'rep', 0, 0, axis_index_groups=PLANE)  30.6 us
    all_to_all x1, blocking collectives, shards(): pieces = last_sum(lax.all_to_all(pieces, 'fsdp', 0, 0), factor)  15 us
    all_to_all x1, blocking collectives, shards(): pieces = sum_copies(lax.all_to_all(right, 'rep', 0, 0), N_FSDP)  13.4 us
    ppermute x2, starting transfers between devices, swap(): return lax.ppermute(x, 'rep', SWAP)  6.59 us
    pallas_call x1, Pallas kernels, final(): call(final_body, 'final', [SMEM] + [VMEM] * 10, [((1, *wide), bf16, ANY),...  4.28 us
    pallas_call x2, Pallas kernels, merge_half(): call(functools.partial(merge_body, flip), 'merge_theirs' if flip else 'me...  3.28 us
    pallas_call x1, Pallas kernels, solve(): call(solve_body, 'solve', [VMEM], [((RANK, RANK), f32, None)], 4, cost=40...  1.74 us
  transfers between devices with their start and end apart: 2, of which 1 were waited for; matrix products, arithmetic and copies ran while one was open for 0% of the time, Pallas kernels for 5%

profile of v6, /device:TPU:1, one launch (start us, length us, event | category | flops | bytes accessed | tf_op | source)
XLA Modules:
  0.0 76.9 jit_solution(1896202981869405518)
XLA Ops:
  0.6 1.3 %merge_theirs.1 = (f32[512,512]{1,0:T(8,128)S(1)}, bf16[512,512]{1,0:T(8,128)(2,1)S(1)}, bf16[512,512]{1,0:T(8,128)(2,1)S(1)}) custom-call(s32[1]{0:T(128)} %bitcast.core, bf16[1,1024,512]{2,1,0:T(8,128)(2,1)} %grads.3, bf16[1,1024,512]{2,1,0:T(8,128)(2,1)} %errors.3), custom_call_target="tpu_custom_call" | custom-call | flops 200000000 | bytes 3125000 | tf_op jit(solution)/shard_map/merge_theirs/pallas_call | solution.py:110
  2.0 3.3 %collective-permute-start = (f32[512,512]{1,0:T(8,128)S(1)}, f32[512,512]{1,0:T(8,128)S(1)}, u32[]{:S(2)}, u32[]{:S(2)}) collective-permute-start(f32[512,512]{1,0:T(8,128)S(1)} %get-tuple-element.24), channel_id=1, source_target_pairs={{0,1},{1,0},{2,3},{3,2},{4,5},{5,4},{6,7},{7,6},{8,9},{9,8},{10,11... | collective-permute-start | bytes 3145736 | tf_op jit(solution)/shard_map/ppermute | solution.py:341
  5.3 1.9 %merge_own.1 = (f32[512,512]{1,0:T(8,128)S(1)}, bf16[512,512]{1,0:T(8,128)(2,1)S(1)}, bf16[512,512]{1,0:T(8,128)(2,1)S(1)}, f32[1024,512]{1,0:T(8,128)S(1)}) custom-call(s32[1]{0:T(128)} %bitcast.core, bf16[1,1024,512]{2,1,0:T(8,128)(2,1)} %grads.3, bf16[1,1024,512]{2,1,0:T(8,128)(2,1)} %errors.3, f32[1024,512]{1,0:T(8,128)} %refs_0_.1), custom_call_target="tpu_custom_call" | custom-call | flops 200000000 | bytes 3125000 | tf_op jit(solution)/shard_map/merge_own/pallas_call | solution.py:110
  7.3 0.3 collective-permute-done.b
  7.6 0.0 copy-start.2
  7.6 0.1 add.6
  7.7 20.8 %all_to_all.20.pieces = f32[16,32,512]{2,1,0:T(8,128)S(1)} all-to-all(f32[16,32,512]{2,1,0:T(8,128)S(1)} %bitcast.4), channel_id=1, replica_groups={{0,2,4,6,8,10,12,14,16,18,20,22,24,26,28,30},{1,3,5,7,9,11,13,15,17,19,..., dimensions={0} | all-to-all | bytes 2097152 | tf_op jit(solution)/shard_map/all_to_all | solution.py:337
  28.5 0.0 copy-done.2
  28.5 0.8 %terms.1 = (f32[16,128]{1,0:T(8,128)S(1)}, f32[32,5,2,128]{3,2,1,0:T(2,128)S(1)}) custom-call(f32[16,32,512]{2,1,0:T(8,128)S(1)} %all_to_all.20.pieces, f32[64,512]{1,0:T(8,128)S(1)} %bitcast.5), custom_call_target="tpu_custom_call" | custom-call | flops 100000000 | bytes 1562500 | tf_op jit(solution)/shard_map/terms/pallas_call | solution.py:165
  29.3 13.4 %all_to_all.21.pieces = f32[32,5,2,128]{3,2,1,0:T(2,128)S(1)} all-to-all(f32[32,5,2,128]{3,2,1,0:T(2,128)S(1)} %get-tuple-element.25), channel_id=1, replica_groups=mesh['fsdp'=8,'rep'=32] {'rep'}, dimensions={0} | all-to-all | bytes 327680 | tf_op jit(solution)/shard_map/all_to_all | solution.py:351
  42.7 0.1 sum_copies.1
  42.7 15.0 %all_to_all.22.pieces = f32[8,5,2,128]{3,2,1,0:T(2,128)S(1)} all-to-all(f32[8,5,2,128]{3,2,1,0:T(2,128)S(1)} %sum_copies.1), channel_id=1, replica_groups=mesh['fsdp'=8,'rep'=32] {'fsdp'}, dimensions={0} | all-to-all | bytes 81920 | tf_op jit(solution)/shard_map/all_to_all | solution.py:352
  57.7 0.1 last_sum.1
  57.8 9.9 %all_to_all.23.sums.sums_own = f32[16,13,2,128]{3,2,1,0:T(2,128)S(1)} all-to-all(f32[16,13,2,128]{3,2,1,0:T(2,128)S(1)} %last_sum.1), channel_id=1, replica_groups={{0,2,4,6,8,10,12,14,16,18,20,22,24,26,28,30},{1,3,5,7,9,11,13,15,17,19,..., dimensions={0} | all-to-all | bytes 425984 | tf_op jit(solution)/shard_map/all_to_all | solution.py:337
  67.6 0.0 copy-start
  67.6 0.0 copy-start.1
  67.6 3.3 %collective-permute-start.1 = (f32[16,13,2,128]{3,2,1,0:T(2,128)S(1)}, f32[16,13,2,128]{3,2,1,0:T(2,128)S(1)}, u32[]{:S(2)}, u32[]{:S(2)}) collective-permute-start(f32[16,13,2,128]{3,2,1,0:T(2,128)S(1)} %all_to_all.23.sums.sums_own), channel_id=1, source_target_pairs={{0,1},{1,0},{2,3},{3,2},{4,5},{5,4},{6,7},{7,6},{8,9},{9,8},{10,11... | collective-permute-start | bytes 638984 | tf_op jit(solution)/shard_map/ppermute | solution.py:341
  70.9 1.7 %solve.1.inverse = f32[64,64]{1,0:T(8,128)S(1)} custom-call(f32[16,13,2,128]{3,2,1,0:T(2,128)S(1)} %all_to_all.23.sums.sums_own), custom_call_target="tpu_custom_call" | custom-call | flops 4000000000 | bytes 62500000 | tf_op jit(solution)/shard_map/solve/pallas_call | solution.py:241
  72.6 0.0 collective-permute-done.1.sums_other
  72.6 0.0 copy-done
  72.6 0.0 copy-done.1
  72.6 4.3 %final.1 = (bf16[1,1024,512]{2,1,0:T(8,128)(2,1)}, f32[64,512]{1,0:T(8,128)}, f32[1024,512]{1,0:T(8,128)}, bf16[1024,512]{1,0:T(8,128)(2,1)}, bf16[1024,512]{1,0:T(8,128)(2,1)}) custom-call(s32[1]{0:T(128)} %bitcast.core, bf16[512,512]{1,0:T(8,128)(2,1)S(1)} %get-tuple-element.19.g_own, bf16[512,512]{1,0:T(8,128)(2,1)S(1)} %get-tuple-element.20.e_own, ...), custom_call_target="tpu_custom_call" | custom-call | flops 400000000 | bytes 6250000 | tf_op jit(solution)/shard_map/final/pallas_call | solution.py:308
Async XLA Ops:
  2.0 5.6 %collective-permute-start = (f32[512,512]{1,0:T(8,128)S(1)}, f32[512,512]{1,0:T(8,128)S(1)}, u32[]{:S(2)}, u32[]{:S(2)}) collective-permute-start(f32[512,512]{1,0:T(8,128)S(1)} %get-tuple-element.24), channel_id=1, source_target_pairs={{0,1},{1,0},{2,3},{3,2},{4,5},{5,4},{6,7},{7,6},{8,9},{9,8},{10,11... | collective-permute-start | bytes 3145736 | tf_op jit(solution)/shard_map/ppermute | solution.py:341
  7.6 20.9 %copy-start.2 = (f32[512,64]{0,1:T(8,128)S(1)}, f32[512,64]{0,1:T(8,128)}, u32[]{:S(2)}) copy-start(f32[512,64]{0,1:T(8,128)} %param.8) | copy-start | bytes 393220
  67.6 5.0 %copy-start = (bf16[1024,512]{1,0:T(8,128)(2,1)S(1)}, bf16[1024,512]{1,0:T(8,128)(2,1)}, u32[]{:S(2)}) copy-start(bf16[1024,512]{1,0:T(8,128)(2,1)} %first.1) | copy-start | bytes 3145732
  67.6 5.0 %copy-start.1 = (bf16[1024,512]{1,0:T(8,128)(2,1)S(1)}, bf16[1024,512]{1,0:T(8,128)(2,1)}, u32[]{:S(2)}) copy-start(bf16[1024,512]{1,0:T(8,128)(2,1)} %second.1) | copy-start | bytes 3145732
  67.6 5.0 %collective-permute-start.1 = (f32[16,13,2,128]{3,2,1,0:T(2,128)S(1)}, f32[16,13,2,128]{3,2,1,0:T(2,128)S(1)}, u32[]{:S(2)}, u32[]{:S(2)}) collective-permute-start(f32[16,13,2,128]{3,2,1,0:T(2,128)S(1)} %all_to_all.23.sums.sums_own), channel_id=1, source_target_pairs={{0,1},{1,0},{2,3},{3,2},{4,5},{5,4},{6,7},{7,6},{8,9},{9,8},{10,11... | collective-permute-start | bytes 638984 | tf_op jit(solution)/shard_map/ppermute | solution.py:341
